TPU v7x, 32 devices: a whole 2x2x4 slice. The times are simulated.
32 devices in a mesh: group: 2 (over y), tile: 4 (over z), strip: 2 (over x), mode: 2 (over core).
Axes of the slice: x: 2, y: 2, z: 4, core: 2. Of those that a mesh axis runs over, the one named last changes fastest.
Arguments:
- object_field: bfloat16 [4, 2, 256, 2048], P('group', 'mode', 'strip', 'tile'), parts along dimension 0, may hold values from -4 to 4
- probe_modes: float32 [4, 2, 128, 128], P('group'), parts along dimension 0, may hold values from -5 to 5
- measured: float32 [4, 32, 128, 128], P(('group', 'strip'), ('tile', 'mode')), parts along dimension 0, may hold values from 0.25 to 16
- pos_tile: int32 [4, 32, 1], P(('group', 'strip')), parts along dimension 0, may hold values from 0 to 3; in each aligned block of 4 rows (0 to 3, 4 to 7, ..., all dimensions but the last counted through in order) at most 2 rows name the same one
- off_row: int32 [4, 32], P(('group', 'strip')), parts along dimension 0, may hold values from 0 to 128, as said below
- off_col: int32 [4, 32], P(('group', 'strip')), parts along dimension 0, may hold values from 0 to 512, as said below
Outputs:
- object_grad: float32 [4, 2, 256, 2048], P('group', 'mode', 'strip', 'tile'), parts along dimension 0
- probe_grad: float32 [4, 2, 128, 128], P('group'), parts along dimension 0
There are 2 independent parts, one for each index of `group`. A program takes and returns all parts, laid end to end along the dimension named above; each array names one. Nothing has to cross between parts.
Inputs may be any that keep to these rules, and one draw needn't show every extreme that they name: `pos_tile`: blocks of 4 consecutive positions belong to one device; within such a block at most 2 positions name the same tile, and in every draw some block has exactly 2 on one tile. `off_row`: each row offset is below 64 or above 64. `off_col`: each column offset is below 64 or above 448.
All inputs are finite; a program needn't handle non-finite values.
Results may differ from a plain program's by a relative error of at most 0.02.
The roundings to bfloat16 on the way count: a program that leaves them out, or rounds other values in their place, can miss the bound.
Values may be sent and summed in bfloat16 or wider, within the bound.
A program may use at most 64 MiB of HBM per device.

v0:
```python
import jax
import jax.numpy as jnp
from jax import lax
from jax.sharding import PartitionSpec as P

prop_phase = 60.0


def with_halo(block, sides, width):
    for axis, dim in sides:
        count = lax.axis_size(axis)
        forward = [(i, i + 1) for i in range(count - 1)]
        backward = [(target, source) for source, target in forward]
        low = lax.ppermute(
            lax.slice_in_dim(block, block.shape[dim] - width, None, axis=dim), axis, forward
        )
        high = lax.ppermute(lax.slice_in_dim(block, 0, width, axis=dim), axis, backward)
        block = jnp.concatenate([low, block, high], axis=dim)
    return block


def dft_tables(length):
    indices = jnp.arange(length, dtype=jnp.int32)
    products = indices[:, None] * indices[None, :] % length
    angles = products.astype(jnp.float32) * (2.0 * jnp.pi / length)
    scale_factor = 1.0 / jnp.sqrt(jnp.float32(length))
    return (
        (jnp.cos(angles) * scale_factor).astype(jnp.bfloat16),
        (-jnp.sin(angles) * scale_factor).astype(jnp.bfloat16),
    )


def propagator(length):
    indices = jnp.arange(length, dtype=jnp.int32)
    shifted = (indices + length // 2) % length - length // 2
    frequency = shifted.astype(jnp.float32) / length
    phases = -prop_phase * (frequency[:, None] ** 2 + frequency[None, :] ** 2)
    return (jnp.cos(phases), jnp.sin(phases))


def make_tables(length):
    cos_table, sin_table = dft_tables(length)
    prop_cos, prop_sin = propagator(length)
    return (cos_table, sin_table, -sin_table, prop_cos, prop_sin)


def right_mult(left, table):
    return jnp.einsum("nij,jk->nik", left, table, preferred_element_type=jnp.float32)


def left_mult(table, right):
    return jnp.einsum("ij,njk->nik", table, right, preferred_element_type=jnp.float32)


def transform(field_re, field_im, cos_table, sin_table):
    half_re = field_re.astype(jnp.bfloat16)
    half_im = field_im.astype(jnp.bfloat16)
    mid_re = (right_mult(half_re, cos_table) - right_mult(half_im, sin_table)).astype(jnp.bfloat16)
    mid_im = (right_mult(half_re, sin_table) + right_mult(half_im, cos_table)).astype(jnp.bfloat16)
    out_re = left_mult(cos_table, mid_re) - left_mult(sin_table, mid_im)
    out_im = left_mult(sin_table, mid_re) + left_mult(cos_table, mid_im)
    return (out_re, out_im)


def position_terms(window, probe_re, probe_im, observed, tables):
    cos_table, sin_table, conj_table, prop_cos, prop_sin = tables
    front_re, front_im = (window[0, 0], window[0, 1])
    rear_re, rear_im = (window[1, 0], window[1, 1])
    wave_a_re = probe_re * front_re - probe_im * front_im
    wave_a_im = probe_re * front_im + probe_im * front_re
    spec_re, spec_im = transform(wave_a_re, wave_a_im, cos_table, sin_table)
    kick_re = spec_re * prop_cos - spec_im * prop_sin
    kick_im = spec_re * prop_sin + spec_im * prop_cos
    inner_re, inner_im = transform(kick_re, kick_im, cos_table, conj_table)
    wave_b_re = inner_re * rear_re - inner_im * rear_im
    wave_b_im = inner_re * rear_im + inner_im * rear_re
    far_re, far_im = transform(wave_b_re, wave_b_im, cos_table, sin_table)
    intensity = jnp.sum(far_re * far_re + far_im * far_im, axis=0)
    amp_factor = 1.0 - jnp.sqrt(observed) / jnp.sqrt(intensity + 1.0)
    back_b_re, back_b_im = transform(
        far_re * amp_factor, far_im * amp_factor, cos_table, conj_table
    )
    grad_in_re = rear_re * back_b_re + rear_im * back_b_im
    grad_in_im = rear_re * back_b_im - rear_im * back_b_re
    back_spec_re, back_spec_im = transform(grad_in_re, grad_in_im, cos_table, sin_table)
    spec_h_re = back_spec_re * prop_cos + back_spec_im * prop_sin
    spec_h_im = back_spec_im * prop_cos - back_spec_re * prop_sin
    back_a_re, back_a_im = transform(spec_h_re, spec_h_im, cos_table, conj_table)
    grad_a_re = jnp.sum(probe_re * back_a_re + probe_im * back_a_im, axis=0)
    grad_a_im = jnp.sum(probe_re * back_a_im - probe_im * back_a_re, axis=0)
    grad_b_re = jnp.sum(inner_re * back_b_re + inner_im * back_b_im, axis=0)
    grad_b_im = jnp.sum(inner_re * back_b_im - inner_im * back_b_re, axis=0)
    pterm_re = front_re * back_a_re + front_im * back_a_im
    pterm_im = front_re * back_a_im - front_im * back_a_re
    gradient_window = jnp.stack(
        [jnp.stack([grad_a_re, grad_a_im]), jnp.stack([grad_b_re, grad_b_im])]
    ).astype(jnp.bfloat16)
    return (gradient_window, jnp.stack([pterm_re, pterm_im]))


def fold_margin(extended, axis_pos, count, width):
    center = lax.slice_in_dim(extended, 2 * width, 2 * width + count, axis=axis_pos)
    upper = lax.slice_in_dim(extended, 0, width, axis=axis_pos)
    lower = lax.slice_in_dim(extended, count + 3 * width, count + 4 * width, axis=axis_pos)
    upper_pad = [(0, 0)] * extended.ndim
    lower_pad = [(0, 0)] * extended.ndim
    upper_pad[axis_pos] = (0, count - width)
    lower_pad[axis_pos] = (count - width, 0)
    return center + jnp.pad(upper, upper_pad) + jnp.pad(lower, lower_pad)


def on_device(object_field, probe_modes, measured, pos_tile, off_row, off_col):
    length = probe_modes.shape[-1]
    margin = length // 2
    tile_rows = object_field.shape[2]
    tile_cols = object_field.shape[3]
    per_dev = measured.shape[1]
    n_tile = lax.axis_size("tile")
    n_mode = lax.axis_size("mode")
    owners = n_tile * n_mode
    slot_count = max(2, 2 * per_dev // n_tile)
    tile_id = lax.axis_index("tile")
    mode_id = lax.axis_index("mode")
    my_block = tile_id * n_mode + mode_id
    tile_list = pos_tile[0, :, 0].reshape(owners, per_dev)
    row_list = off_row[0].reshape(owners, per_dev)
    col_list = off_col[0].reshape(owners, per_dev)
    slot_order = jnp.arange(per_dev, dtype=jnp.int32)
    same_tile = (tile_list[:, :, None] == tile_list[:, None, :]) & (
        slot_order[None, None, :] < slot_order[None, :, None]
    )
    slot_rank = jnp.sum(same_tile.astype(jnp.int32), axis=2)
    my_tiles = lax.dynamic_index_in_dim(tile_list, my_block, 0, keepdims=False)
    my_rank = lax.dynamic_index_in_dim(slot_rank, my_block, 0, keepdims=False)
    slice_ids = jnp.arange(n_mode, dtype=jnp.int32)
    padded = with_halo(object_field, (("tile", 3), ("strip", 2)), margin)
    tables = make_tables(length)
    probe_re = probe_modes[0]
    probe_im = probe_modes[1]
    slot_ids = jnp.arange(slot_count, dtype=jnp.int32)
    chosen = (
        (tile_list == tile_id)[:, None, :] & (slot_rank[:, None, :] == slot_ids[None, :, None])
    ).astype(jnp.int32)
    send_rows = jnp.sum(chosen * row_list[:, None, :], axis=2).reshape(-1)
    send_cols = jnp.sum(chosen * col_list[:, None, :], axis=2).reshape(-1)
    filled = jnp.sum(chosen, axis=2).reshape(-1)
    padded_obj = padded[:, 0]

    def crop_window(row_at, col_at, keep):
        window = lax.dynamic_slice(padded_obj, (0, row_at, col_at), (2, length, length))
        return window * keep.astype(jnp.bfloat16)

    outgoing = jax.vmap(crop_window)(send_rows, send_cols, filled).reshape(
        owners, slot_count, 2, length, length
    )
    arrived = lax.all_to_all(outgoing, ("tile", "mode"), split_axis=0, concat_axis=0, tiled=True)
    source = my_tiles[:, None] * n_mode + slice_ids[None, :]
    windows = arrived[source, my_rank[:, None]]

    def advance(running, inputs):
        window, observed = inputs
        gradient_window, pterm = position_terms(
            window.astype(jnp.float32), probe_re, probe_im, observed, tables
        )
        return (running + pterm, gradient_window)

    probe_part, gradients = lax.scan(
        advance, jnp.zeros(probe_modes.shape, jnp.float32), (windows, measured[0])
    )
    back_buf = jnp.zeros((n_tile, n_mode, slot_count, 2, length, length), jnp.bfloat16)
    back_buf = back_buf.at[my_tiles[:, None], slice_ids[None, :], my_rank[:, None]].set(gradients)
    returned = lax.all_to_all(
        back_buf.reshape(owners, slot_count, 2, length, length),
        ("tile", "mode"),
        split_axis=0,
        concat_axis=0,
        tiled=True,
    )
    returned = returned.reshape(owners * slot_count, 2, length, length)

    def add_window(position, grid_one):
        addend = returned[position].astype(jnp.float32)
        row_at = send_rows[position]
        col_at = send_cols[position]
        current = lax.dynamic_slice(grid_one, (0, row_at, col_at), (2, length, length))
        return lax.dynamic_update_slice(grid_one, current + addend, (0, row_at, col_at))

    start_grid = jnp.zeros((2, tile_rows + 2 * margin, tile_cols + 2 * margin), jnp.float32)
    grad_grid = lax.fori_loop(0, owners * slot_count, add_window, start_grid)
    extended = with_halo(
        grad_grid.astype(jnp.bfloat16), (("tile", 2), ("strip", 1)), margin
    ).astype(grad_grid.dtype)
    folded = fold_margin(extended, 1, tile_rows, margin)
    folded = fold_margin(folded, 2, tile_cols, margin)
    object_grad = folded[:, None]
    probe_grad = lax.psum(probe_part, ("tile", "strip", "mode"))
    return (object_grad, probe_grad)


def solution(mesh):
    return jax.shard_map(
        on_device,
        mesh=mesh,
        in_specs=(
            P("group", "mode", "strip", "tile"),
            P("group", None, None, None),
            P(("group", "strip"), ("tile", "mode"), None, None),
            P(("group", "strip"), None, None),
            P(("group", "strip"), None),
            P(("group", "strip"), None),
        ),
        out_specs=(P("group", "mode", "strip", "tile"), P("group", None, None, None)),
        check_vma=False,
    )
```

profile of v0, /device:TPU:0, one launch (start us, length us, event | category | flops | bytes accessed | tf_op | source)
XLA Modules:
  0.0 440.0 jit_solution(472911169141362270)
XLA Ops:
  7.2 1.0 fusion.394
  8.2 4.9 %collective-permute-start = (bf16[2,1,128,64]{3,2,0,1:T(8,128)(2,1)S(1)}, bf16[2,1,128,64]{3,2,0,1:T(8,128)(2,1)S(1)}, u32[]{:S(2)}, u32[]{:S(2)}) collective-permute-start(bf16[2,1,128,64]{3,2,0,1:T(8,128)(2,1)S(1)} %get-tuple-element.617), channel_id=1, source_target_pairs={{0,4},{4,8},{8,12},{1,5},{5,9},{9,13},{2,6},{6,10},{10,14},{3,7},{... | collective-permute-start | bytes 98312 | tf_op jit(solution)/shard_map/ppermute | solution.py:14
  13.1 1.3 collective-permute-start.1
  15.0 1.3 reduce.11
  16.5 1.3 reduce.12
  18.0 1.3 reduce.13
  20.0 1.1 pad_maximum_fusion
  21.2 3.4 collective-permute-start.2
  24.6 1.3 collective-permute-start.3
  26.0 1.7 collective-permute-done.2
  27.7 4.1 collective-permute-done.3
  32.1 31.1 %while.31 = (s32[]{:T(128)}, bf16[2,256,640]{2,1,0:T(8,128)(2,1)S(1)}, s32[16,3]{0,1:T(4,128)S(1)}, bf16[16,2,128,128]{3,2,1,0:T(8,128)(2,1)S(1)}, s32[]{:T(128)}) while((s32[]{:T(128)}, bf16[2,256,640]{2,1,0:T(8,128)(2,1)S(1)}, s32[16,3]{0,1:T(4,128)S(1)}, bf16[16,2,128,128]{3,2,1,0:T(8,128)(2,1)S(1)}, s32[]{:T(128)}) %tuple.128), condition=%wide.while_cond, body=%wide.while_body.sunk | while | flops 2 | bytes 131189 | solution.py:150
  32.7 1.3 bitcast_dynamic-update-slice_fusion.2
  34.6 1.3 bitcast_dynamic-update-slice_fusion.2
  36.5 1.3 bitcast_dynamic-update-slice_fusion.2
  38.5 1.3 bitcast_dynamic-update-slice_fusion.2
  40.4 1.3 bitcast_dynamic-update-slice_fusion.2
  42.4 1.3 bitcast_dynamic-update-slice_fusion.2
  44.3 1.3 bitcast_dynamic-update-slice_fusion.2
  46.3 1.3 bitcast_dynamic-update-slice_fusion.2
  48.2 1.3 bitcast_dynamic-update-slice_fusion.2
  50.1 1.3 bitcast_dynamic-update-slice_fusion.2
  52.1 1.3 bitcast_dynamic-update-slice_fusion.2
  54.0 1.3 bitcast_dynamic-update-slice_fusion.2
  56.0 1.3 bitcast_dynamic-update-slice_fusion.2
  57.9 1.3 bitcast_dynamic-update-slice_fusion.2
  59.8 1.3 bitcast_dynamic-update-slice_fusion.2
  61.8 1.3 bitcast_dynamic-update-slice_fusion.2
  63.1 1.1 broadcast_multiply_fusion
  64.3 6.0 %all-to-all-start = ((bf16[8,2,2,128,128]{4,3,2,1,0:T(8,128)(2,1)}), bf16[8,2,2,128,128]{4,3,2,1,0:T(8,128)(2,1)S(1)}, u32[]{:S(2)}, u32[]{:S(2)}) async-start(bf16[8,2,2,128,128]{4,3,2,1,0:T(8,128)(2,1)} %broadcast_multiply_fusion), calls=%async_computation | async-start | bytes 2097152 | tf_op jit(solution)/shard_map/all_to_all | solution.py:156
  71.2 25.7 %all-to-all-done = bf16[8,2,2,128,128]{4,3,2,1,0:T(8,128)(2,1)S(1)} async-done(((bf16[8,2,2,128,128]{4,3,2,1,0:T(8,128)(2,1)}), bf16[8,2,2,128,128]{4,3,2,1,0:T(8,128)(2,1)S(1)}, u32[]{:S(2)}, u32[]{:S(2)}) %all-to-all-start) | async-done | bytes 1048608 | tf_op jit(solution)/shard_map/all_to_all | solution.py:156
  97.5 81.9 %while.32 = (s32[]{:T(128)}, f32[2,2,128,128]{2,3,1,0:T(8,128)S(1)}, bf16[4,2,2,128,128]{3,4,2,1,0:T(8,128)(2,1)S(1)}, bf16[4,2,2,128,128]{4,3,2,1,0:T(8,128)(2,...) while((s32[]{:T(128)}, ...), condition=%wide.region_10.11_spmd.clone.clone.clone.clone, body=%wide.region_4.10_spmd.clone.clone.clone.clone.sunk | while | flops 420413440 | bytes 18350712 | solution.py:167
  179.7 1.2 broadcast_in_dim.22
  180.9 2.6 scatter_fusion
  183.5 3.6 all-to-all-start.1
  187.3 26.3 %all-to-all-done.1 = bf16[8,2,2,128,128]{4,3,2,1,0:T(8,128)(2,1)S(1)} async-done(((bf16[8,2,2,128,128]{4,3,2,1,0:T(8,128)(2,1)}), bf16[8,2,2,128,128]{4,3,2,1,0:T(8,128)(2,1)S(1)}, u32[]{:S(2)}, u32[]{:S(2)}) %all-to-all-start.1) | async-done | bytes 1048608 | tf_op jit(solution)/shard_map/all_to_all | solution.py:172
  213.7 114.9 %while.30 = (s32[]{:T(128)}, f32[2,256,640]{2,1,0:T(8,128)S(1)}, s32[16]{0:T(128)S(1)}, s32[16]{0:T(128)S(1)}, bf16[16,2,128,128]{3,2,1,0:T(8,128)(2,1)S(1)}, /*index=5*/s32[]{:T(128)}, s32[]{:T(128)}, s32[]{:T(128)}, s32[]{:T(128)}) while((s32[]{:T(128)}, f32[2,256,640]{2,1,0:T(8,128)S(1)}, s32[16]{0:T(128)S(1)}, s32[16]{0:T(128)S(1)}, ...), condition=%wide.region_13.14_spmd, body=%wide.region_12.13_spmd.sunk | while | flops 65544 | bytes 590025 | solution.py:189
  218.9 2.3 dynamic_update_slice.18
  226.4 1.7 dynamic_update_slice.18
  233.3 2.5 dynamic_update_slice.18
  241.0 1.7 dynamic_update_slice.18
  248.0 2.4 dynamic_update_slice.18
  255.5 1.7 dynamic_update_slice.18
  262.5 2.4 dynamic_update_slice.18
  270.1 1.7 dynamic_update_slice.18
  277.0 2.2 dynamic_update_slice.18
  284.4 1.7 dynamic_update_slice.18
  291.3 1.7 dynamic_update_slice.18
  298.2 1.7 dynamic_update_slice.18
  305.2 2.2 dynamic_update_slice.18
  312.6 1.7 dynamic_update_slice.18
  319.5 2.1 dynamic_update_slice.18
  326.9 1.7 dynamic_update_slice.18
  328.8 1.5 collective-permute-start.4
  330.3 1.3 collective-permute-start.5
  331.6 1.7 collective-permute-done.4
  333.3 4.1 collective-permute-done.5
  337.6 2.3 collective-permute-start.6
  340.0 1.3 collective-permute-start.7
  342.1 1.0 collective-permute-done.6
  343.2 4.4 collective-permute-done.7
  348.9 0.9 fusion.374
  349.8 81.7 %all-reduce.4.cloned.1.call-done = f32[2,2,128,128]{3,2,1,0:T(8,128)} async-done(((f32[2,2,128,128]{3,2,1,0:T(8,128)}), f32[2,2,128,128]{3,2,1,0:T(8,128)}) %all-reduce.4.cloned.1.call-update) | async-done | bytes 262160 | tf_op jit(solution)/shard_map/psum | solution.py:196
  431.5 1.7 copy.445
  (377 shorter events, 116.8 us)
Async XLA Ops:
  7.2 24.7 %copy-start = (bf16[2,1,128,512]{3,2,1,0:T(8,128)(2,1)S(1)}, bf16[2,1,128,512]{3,2,1,0:T(8,128)(2,1)}, u32[]{:S(2)}) copy-start(bf16[2,1,128,512]{3,2,1,0:T(8,128)(2,1)} %param.10) | copy-start | bytes 786436
  8.2 11.8 %collective-permute-start = (bf16[2,1,128,64]{3,2,0,1:T(8,128)(2,1)S(1)}, bf16[2,1,128,64]{3,2,0,1:T(8,128)(2,1)S(1)}, u32[]{:S(2)}, u32[]{:S(2)}) collective-permute-start(bf16[2,1,128,64]{3,2,0,1:T(8,128)(2,1)S(1)} %get-tuple-element.617), channel_id=1, source_target_pairs={{0,4},{4,8},{8,12},{1,5},{5,9},{9,13},{2,6},{6,10},{10,14},{3,7},{... | collective-permute-start | bytes 98312 | tf_op jit(solution)/shard_map/ppermute | solution.py:14
  13.1 6.9 %collective-permute-start.1 = (bf16[2,1,128,64]{3,2,0,1:T(8,128)(2,1)S(1)}, bf16[2,1,128,64]{3,2,0,1:T(8,128)(2,1)S(1)}, u32[]{:S(2)}, u32[]{:S(2)}) collective-permute-start(bf16[2,1,128,64]{3,2,0,1:T(8,128)(2,1)S(1)} %get-tuple-element.618), channel_id=1, source_target_pairs={{4,0},{8,4},{12,8},{5,1},{9,5},{13,9},{6,2},{10,6},{14,10},{7,3},{... | collective-permute-start | bytes 98312 | tf_op jit(solution)/shard_map/ppermute | solution.py:17
  21.2 6.6 %collective-permute-start.2 = (bf16[2,1,64,640]{3,2,0,1:T(8,128)(2,1)S(1)}, bf16[2,1,64,640]{3,2,0,1:T(8,128)(2,1)S(1)}, u32[]{:S(2)}, u32[]{:S(2)}) collective-permute-start(bf16[2,1,64,640]{3,2,0,1:T(8,128)(2,1)S(1)} %get-tuple-element.613), channel_id=1, source_target_pairs={{0,2},{1,3},{4,6},{5,7},{8,10},{9,11},{12,14},{13,15},{16,18},{17,... | collective-permute-start | bytes 491528 | tf_op jit(solution)/shard_map/ppermute | solution.py:14
  24.6 7.3 %collective-permute-start.3 = (bf16[2,1,64,640]{3,2,0,1:T(8,128)(2,1)S(1)}, bf16[2,1,64,640]{3,2,0,1:T(8,128)(2,1)S(1)}, u32[]{:S(2)}, u32[]{:S(2)}) collective-permute-start(bf16[2,1,64,640]{3,2,0,1:T(8,128)(2,1)S(1)} %get-tuple-element.614), channel_id=1, source_target_pairs={{2,0},{3,1},{6,4},{7,5},{10,8},{11,9},{14,12},{15,13},{18,16},{19,... | collective-permute-start | bytes 491528 | tf_op jit(solution)/shard_map/ppermute | solution.py:17
  64.3 6.4 %copy-start.1 = (f32[2,2,128,128]{3,2,1,0:T(8,128)S(1)}, f32[2,2,128,128]{3,2,1,0:T(8,128)}, u32[]{:S(2)}) copy-start(f32[2,2,128,128]{3,2,1,0:T(8,128)} %param.11) | copy-start | bytes 786436
  64.3 6.7 %copy-start.2 = (f32[1,4,128,128]{3,2,1,0:T(8,128)S(1)}, f32[1,4,128,128]{3,2,1,0:T(8,128)}, u32[]{:S(2)}) copy-start(f32[1,4,128,128]{3,2,1,0:T(8,128)} %param.12) | copy-start | bytes 786436
  64.3 32.6 %all-to-all-start = ((bf16[8,2,2,128,128]{4,3,2,1,0:T(8,128)(2,1)}), bf16[8,2,2,128,128]{4,3,2,1,0:T(8,128)(2,1)S(1)}, u32[]{:S(2)}, u32[]{:S(2)}) async-start(bf16[8,2,2,128,128]{4,3,2,1,0:T(8,128)(2,1)} %broadcast_multiply_fusion), calls=%async_computation | async-start | bytes 2097152 | tf_op jit(solution)/shard_map/all_to_all | solution.py:156
  183.5 30.1 %all-to-all-start.1 = ((bf16[8,2,2,128,128]{4,3,2,1,0:T(8,128)(2,1)}), bf16[8,2,2,128,128]{4,3,2,1,0:T(8,128)(2,1)S(1)}, u32[]{:S(2)}, u32[]{:S(2)}) async-start(bf16[8,2,2,128,128]{4,3,2,1,0:T(8,128)(2,1)} %bitcast.14), calls=%async_computation.1 | async-start | bytes 2097152 | tf_op jit(solution)/shard_map/all_to_all | solution.py:172
  187.1 244.4 %all-reduce.4.cloned.1.call-start = ((), (), s32[]{:S(2)}) async-start(), calls=%async_computation.2 | async-start | bytes 524288 | tf_op jit(solution)/shard_map/psum | solution.py:196
  328.8 4.5 %collective-permute-start.4 = (bf16[2,256,64]{2,1,0:T(8,128)(2,1)S(1)}, bf16[2,256,64]{2,1,0:T(8,128)(2,1)S(1)}, u32[]{:S(2)}, u32[]{:S(2)}) collective-permute-start(bf16[2,256,64]{2,1,0:T(8,128)(2,1)S(1)} %get-tuple-element.611), channel_id=1, source_target_pairs={{0,4},{4,8},{8,12},{1,5},{5,9},{9,13},{2,6},{6,10},{10,14},{3,7},{... | collective-permute-start | bytes 196616 | tf_op jit(solution)/shard_map/ppermute | solution.py:14
  330.3 7.1 %collective-permute-start.5 = (bf16[2,256,64]{2,1,0:T(8,128)(2,1)S(1)}, bf16[2,256,64]{2,1,0:T(8,128)(2,1)S(1)}, u32[]{:S(2)}, u32[]{:S(2)}) collective-permute-start(bf16[2,256,64]{2,1,0:T(8,128)(2,1)S(1)} %get-tuple-element.612), channel_id=1, source_target_pairs={{4,0},{8,4},{12,8},{5,1},{9,5},{13,9},{6,2},{10,6},{14,10},{7,3},{... | collective-permute-start | bytes 196616 | tf_op jit(solution)/shard_map/ppermute | solution.py:17
  337.6 5.5 %collective-permute-start.6 = (bf16[2,64,768]{2,1,0:T(8,128)(2,1)S(1)}, bf16[2,64,768]{2,1,0:T(8,128)(2,1)S(1)}, u32[]{:S(2)}, u32[]{:S(2)}) collective-permute-start(bf16[2,64,768]{2,1,0:T(8,128)(2,1)S(1)} %get-tuple-element.609), channel_id=1, source_target_pairs={{0,2},{1,3},{4,6},{5,7},{8,10},{9,11},{12,14},{13,15},{16,18},{17,... | collective-permute-start | bytes 589832 | tf_op jit(solution)/shard_map/ppermute | solution.py:14
  340.0 7.6 %collective-permute-start.7 = (bf16[2,64,768]{2,1,0:T(8,128)(2,1)S(1)}, bf16[2,64,768]{2,1,0:T(8,128)(2,1)S(1)}, u32[]{:S(2)}, u32[]{:S(2)}) collective-permute-start(bf16[2,64,768]{2,1,0:T(8,128)(2,1)S(1)} %get-tuple-element.610), channel_id=1, source_target_pairs={{2,0},{3,1},{6,4},{7,5},{10,8},{11,9},{14,12},{15,13},{18,16},{19,... | collective-permute-start | bytes 589832 | tf_op jit(solution)/shard_map/ppermute | solution.py:17
  347.6 0.7 copy-start.4
  348.2 0.7 copy-start.3
Sparse Core Ops, SparseCore 0:
  342.3 89.1 all-reduce.3
where the time goes:
time: 442 us; the launch traced here: 440 us
  waiting for transfers between devices  151 us (34%)
  local copies, waits for them, and re-layouts  93.5 us (21%)
  matrix products  77.4 us (18%)
  loops' own time  64.6 us (15%)
  starting transfers between devices  27 us (6%)
  between operations  14.4 us (3%)
  other arithmetic  12.4 us (3%)
    psum x1, waiting for transfers between devices, on_device(): probe_grad = lax.psum(probe_part, ('tile', 'strip', 'mode'))  81.7 us
    another operation x1, loops' own time, on_device(): grad_grid = lax.fori_loop(0, owners * slot_count, add_window, start_grid)  62.7 us
    dot_general x96, matrix products, left_mult(): jnp.einsum('ij,njk->nik', table, right, preferred_element_type=jnp.float32)  39.1 us
    dot_general x96, matrix products, right_mult(): jnp.einsum('nij,jk->nik', left, table, preferred_element_type=jnp.float32)  38.3 us
    dynamic_update_slice x16, local copies, waits for them, and re-layouts, add_window(): lax.dynamic_update_slice(grid_one, current + addend, (0, row_at, col_at))  31.6 us
    gather x48, local copies, waits for them, and re-layouts  30.8 us
    all_to_all x1, waiting for transfers between devices, on_device(): lax.all_to_all(back_buf.reshape(owners, slot_count, 2, length, length), (...  26.3 us
    all_to_all x1, waiting for transfers between devices, on_device(): lax.all_to_all(outgoing, ('tile', 'mode'), split_axis=0, concat_axis=0, t...  25.7 us
  transfers between devices with their start and end apart: 11, of which 9 were waited for; matrix products, arithmetic and copies ran while one was open for 2% of the time, Pallas kernels for 0%

commit v1 on v0

v1 whole, which is shorter than its diff:
```python
import jax
import jax.numpy as jnp
import numpy as np
from jax import lax
from jax.experimental import pallas as pl
from jax.experimental.pallas import tpu as pltpu
from jax.sharding import PartitionSpec as P

prop_phase = 60.0
vmem_bytes = 48 * 1024 * 1024
f32 = jnp.float32
bf16 = jnp.bfloat16


def make_tables(length):
    indices = np.arange(length)
    angles = (indices[:, None] * indices[None, :] % length) * (2.0 * np.pi / length)
    cos = (np.cos(angles) / np.sqrt(length)).astype(np.float32)
    sin = (-np.sin(angles) / np.sqrt(length)).astype(np.float32)
    forward = np.block([[cos, sin], [-sin, cos]])
    inverse = np.block([[cos, -sin], [sin, cos]])
    shifted = (indices + length // 2) % length - length // 2
    frequency = shifted / length
    phases = -prop_phase * (frequency[:, None] ** 2 + frequency[None, :] ** 2)
    return (
        jnp.asarray(np.stack([forward, inverse])).astype(bf16),
        jnp.asarray(np.stack([np.cos(phases), np.sin(phases)]).astype(np.float32)),
    )


def with_halo(block, sides, width):
    for axis, dim in sides:
        count = lax.axis_size(axis)
        forward = [(i, i + 1) for i in range(count - 1)]
        backward = [(target, source) for source, target in forward]
        low = lax.ppermute(
            lax.slice_in_dim(block, block.shape[dim] - width, None, axis=dim), axis, forward
        )
        high = lax.ppermute(lax.slice_in_dim(block, 0, width, axis=dim), axis, backward)
        block = jnp.concatenate([low, block, high], axis=dim)
    return block


def ranks(tile_ref, first, per_dev):
    tiles = [tile_ref[first + q] for q in range(per_dev)]
    out = []
    for q in range(per_dev):
        rank = jnp.int32(0)
        for earlier in range(q):
            rank = rank + jnp.where(tiles[earlier] == tiles[q], 1, 0)
        out.append(rank)
    return tiles, out


def slot_place(refs, owner, slot, tile, per_dev):
    tile_ref, row_ref, col_ref = refs
    first = owner * per_dev
    tiles, order = ranks(tile_ref, first, per_dev)
    row, col, keep = jnp.int32(0), jnp.int32(0), jnp.int32(0)
    for q in range(per_dev):
        hit = jnp.where((tiles[q] == tile) & (order[q] == slot), 1, 0)
        row = row + hit * row_ref[first + q]
        col = col + hit * col_ref[first + q]
        keep = keep + hit
    return row, col, keep


def one_hot(shape, dim, shift, keep=None):
    wide = lax.broadcasted_iota(jnp.int32, shape, dim)
    narrow = lax.broadcasted_iota(jnp.int32, shape, 1 - dim)
    hit = wide == narrow + shift
    if keep is not None:
        hit = hit & (keep > 0)
    return jnp.where(hit, 1.0, 0.0).astype(bf16)


def dot(a, b):
    return jnp.dot(a, b, preferred_element_type=f32)


def column_base(col, width, length):
    return jnp.minimum(col // length * length, width - 2 * length)


def crop_kernel(per_dev, slots, tile_ref, row_ref, col_ref, padded_ref, out_ref):
    tile = lax.axis_index("tile")
    length = out_ref.shape[-1]
    _, rows, width = padded_ref.shape

    def body(index, carry):
        owner, slot = index // slots, index % slots
        row, col, _ = slot_place((tile_ref, row_ref, col_ref), owner, slot, tile, per_dev)
        base = column_base(col, width, length)
        pick_row = one_hot((length, rows), 1, row)
        pick_col = one_hot((2 * length, length), 0, col - base)
        for part in range(2):
            block = padded_ref[part, :, pl.ds(pl.multiple_of(base, length), 2 * length)]
            out_ref[index, part] = dot(dot(pick_row, block).astype(bf16), pick_col).astype(bf16)
        return carry

    lax.fori_loop(0, out_ref.shape[0], body, 0)


def scatter_kernel(per_dev, slots, tile_ref, row_ref, col_ref, back_ref, grid_ref):
    tile = lax.axis_index("tile")
    length = back_ref.shape[-1]
    _, rows, width = grid_ref.shape
    grid_ref[...] = jnp.zeros_like(grid_ref)

    def body(index, carry):
        owner, slot = index // slots, index % slots
        row, col, keep = slot_place((tile_ref, row_ref, col_ref), owner, slot, tile, per_dev)
        base = column_base(col, width, length)

        @pl.when(keep > 0)
        def _():
            put_row = one_hot((rows, length), 0, row)
            put_col = one_hot((length, 2 * length), 1, col - base)
            for part in range(2):
                where = pl.ds(pl.multiple_of(base, length), 2 * length)
                spread = dot(put_row, back_ref[index, part]).astype(bf16)
                grid_ref[part, :, where] += dot(spread, put_col)

        return carry

    lax.fori_loop(0, back_ref.shape[0], body, 0)


def split(field, length):
    modes = field.shape[1] // length
    return [
        (field[:length, m * length : (m + 1) * length], field[length:, m * length : (m + 1) * length])
        for m in range(modes)
    ]


def transform(fields, right, left, length):
    packed = jnp.concatenate(
        [jnp.concatenate([re.astype(bf16), im.astype(bf16)], axis=1) for re, im in fields], axis=0
    )
    mid = dot(packed, right).astype(bf16)
    turned = jnp.concatenate(
        [
            jnp.concatenate(
                [mid[m * length : (m + 1) * length, c * length : (c + 1) * length] for m in range(len(fields))],
                axis=1,
            )
            for c in range(2)
        ],
        axis=0,
    )
    return split(dot(left, turned), length)


def mul(a, b):
    return (a[0] * b[0] - a[1] * b[1], a[0] * b[1] + a[1] * b[0])


def conj_mul(a, b):
    return (a[0] * b[0] + a[1] * b[1], a[0] * b[1] - a[1] * b[0])


def total(pairs):
    return (sum(p[0] for p in pairs[1:]) + pairs[0][0], sum(p[1] for p in pairs[1:]) + pairs[0][1])


def position_terms(front, rear, probes, observed, tables, prop):
    length = observed.shape[0]
    ahead, behind = tables
    forward = lambda f: transform(f, ahead, behind, length)
    inverse = lambda f: transform(f, behind, ahead, length)
    spec = forward([mul(p, front) for p in probes])
    inner = inverse([mul(s, prop) for s in spec])
    far = forward([mul(s, rear) for s in inner])
    intensity = sum(re * re + im * im for re, im in far[1:]) + far[0][0] ** 2 + far[0][1] ** 2
    factor = 1.0 - jnp.sqrt(observed) / jnp.sqrt(intensity + 1.0)
    back_b = inverse([(re * factor, im * factor) for re, im in far])
    back_spec = forward([conj_mul(rear, b) for b in back_b])
    back_a = inverse([conj_mul(prop, b) for b in back_spec])
    grad_a = total([conj_mul(p, b) for p, b in zip(probes, back_a)])
    grad_b = total([conj_mul(s, b) for s, b in zip(inner, back_b)])
    return grad_a, grad_b, [conj_mul(front, b) for b in back_a]


def position_kernel(n_tile, n_mode, slots, tile_ref, arrived_ref, probe_ref, meas_ref, table_ref, prop_ref, back_ref, pgrad_ref):
    per_dev = meas_ref.shape[0]
    modes = probe_ref.shape[1]
    owner = lax.axis_index("tile") * n_mode + lax.axis_index("mode")
    tiles, order = ranks(tile_ref, owner * per_dev, per_dev)
    tables = (table_ref[0], table_ref[1])
    for q in range(per_dev):
        place = [(tiles[q] * n_mode + k * n_mode // 2) * slots + order[q] for k in range(2)]
        pair = lambda k: (arrived_ref[place[k], 0].astype(f32), arrived_ref[place[k], 1].astype(f32))
        probes = [(probe_ref[0, m], probe_ref[1, m]) for m in range(modes)]
        grad_a, grad_b, terms = position_terms(
            pair(0), pair(1), probes, meas_ref[q], tables, (prop_ref[0], prop_ref[1])
        )
        for k, grad in enumerate((grad_a, grad_b)):
            for part in range(2):
                back_ref[place[k], part] = grad[part].astype(bf16)
        for m, term in enumerate(terms):
            for part in range(2):
                if q == 0:
                    pgrad_ref[part, m] = term[part]
                else:
                    pgrad_ref[part, m] += term[part]


smem = pl.BlockSpec(memory_space=pltpu.SMEM)
vmem = pl.BlockSpec(memory_space=pltpu.VMEM)
params = pltpu.CompilerParams(vmem_limit_bytes=vmem_bytes)


def on_device(object_field, probe_modes, measured, pos_tile, off_row, off_col):
    length = probe_modes.shape[-1]
    margin = length // 2
    tile_rows = object_field.shape[2]
    tile_cols = object_field.shape[3]
    per_dev = measured.shape[1]
    n_tile = lax.axis_size("tile")
    n_mode = lax.axis_size("mode")
    slots = max(2, 2 * per_dev // n_tile)
    owners = n_tile * n_mode
    count = owners * slots
    tables, prop = make_tables(length)
    places = (pos_tile[0, :, 0], off_row[0], off_col[0])
    padded = with_halo(object_field[:, 0], (("tile", 2), ("strip", 1)), margin)
    windows = jax.ShapeDtypeStruct((count, 2, length, length), bf16)
    outgoing = pl.pallas_call(
        lambda *refs: crop_kernel(per_dev, slots, *refs),
        out_shape=windows,
        in_specs=[smem] * 3 + [vmem],
        out_specs=vmem,
        compiler_params=params,
        name="crop",
    )(*places, padded)
    arrived = lax.all_to_all(outgoing, ("tile", "mode"), split_axis=0, concat_axis=0, tiled=True)
    back, probe_part = pl.pallas_call(
        lambda *refs: position_kernel(n_tile, n_mode, slots, *refs),
        out_shape=(windows, jax.ShapeDtypeStruct(probe_modes.shape, f32)),
        in_specs=[smem] + [vmem] * 5,
        out_specs=(vmem, vmem),
        compiler_params=params,
        name="positions",
    )(places[0], arrived, probe_modes, measured[0], tables, prop)
    probe_grad = lax.psum(probe_part, ("tile", "strip", "mode"))
    returned = lax.all_to_all(back, ("tile", "mode"), split_axis=0, concat_axis=0, tiled=True)
    grid = pl.pallas_call(
        lambda *refs: scatter_kernel(per_dev, slots, *refs),
        out_shape=jax.ShapeDtypeStruct((2, tile_rows + 2 * margin, tile_cols + 2 * margin), f32),
        in_specs=[smem] * 3 + [vmem],
        out_specs=vmem,
        compiler_params=params,
        name="scatter",
    )(*places, returned)
    folded = fold(grid, "tile", 2, tile_cols, margin)
    folded = fold(folded, "strip", 1, tile_rows, margin)
    return (folded[:, None], probe_grad)


def fold(grid, axis, dim, count, width):
    steps = lax.axis_size(axis)
    forward = [(i, i + 1) for i in range(steps - 1)]
    backward = [(target, source) for source, target in forward]
    cut = lambda lo, hi: lax.slice_in_dim(grid, lo, hi, axis=dim)
    low = lax.ppermute(cut(count + width, count + 2 * width).astype(bf16), axis, forward)
    high = lax.ppermute(cut(0, width).astype(bf16), axis, backward)
    low_pad = [(0, 0)] * grid.ndim
    high_pad = [(0, 0)] * grid.ndim
    low_pad[dim] = (0, count - width)
    high_pad[dim] = (count - width, 0)
    return (
        cut(width, width + count)
        + jnp.pad(low.astype(f32), low_pad)
        + jnp.pad(high.astype(f32), high_pad)
    )


def solution(mesh):
    return jax.shard_map(
        on_device,
        mesh=mesh,
        in_specs=(
            P("group", "mode", "strip", "tile"),
            P("group", None, None, None),
            P(("group", "strip"), ("tile", "mode"), None, None),
            P(("group", "strip"), None, None),
            P(("group", "strip"), None),
            P(("group", "strip"), None),
        ),
        out_specs=(P("group", "mode", "strip", "tile"), P("group", None, None, None)),
        check_vma=False,
    )
```

time: 442 us -> 223 us (0.50)
  local copies, waits for them, and re-layouts: 93.5 us -> 2.87 us
  matrix products: 77.4 us -> 0 us
  loops' own time: 64.6 us -> 0 us
  blocking collectives: 0 us -> 59.4 us
  waiting for transfers between devices: 151 us -> 105 us
  Pallas kernels: 0 us -> 21.6 us
  other arithmetic: 12.4 us -> 2.65 us
  starting transfers between devices: 27 us -> 17.3 us
    dot_general x192 -> x0, matrix products: 77.4 us -> none  [the longest x96 39.1 us: left_mult(): jnp.einsum('ij,njk->nik', table, right, preferred_element_type=jnp.float32)]
    another operation x3 -> x0, loops' own time: 64.6 us -> none  [the longest x1 62.7 us: on_device(): grad_grid = lax.fori_loop(0, owners * slot_count, add_window, start_grid)]
    all_to_all x0 -> x2, blocking collectives: none -> 59.4 us  [the longest x1 30.4 us: on_device(): lax.all_to_all(outgoing, ('tile', 'mode'), split_axis=0, concat_axis=0, t...]
    all_to_all x2 -> x0, waiting for transfers between devices: 52 us -> none  [the longest x1 26.3 us: on_device(): lax.all_to_all(back_buf.reshape(owners, slot_count, 2, length, length), (...]
    dynamic_update_slice x16 -> x0, local copies, waits for them, and re-layouts: 31.6 us -> none  [add_window(): lax.dynamic_update_slice(grid_one, current + addend, (0, row_at, col_at))]
    gather x49 -> x0, local copies, waits for them, and re-layouts: 31.5 us -> none
    pallas_call x0 -> x3, Pallas kernels: none -> 21.6 us  [the longest x1 9.31 us: on_device(): pl.pallas_call(lambda *refs: position_kernel(n_tile, n_mode, slots, *refs...]
    dynamic_slice x41 -> x0, local copies, waits for them, and re-layouts: 19.6 us -> none  [the longest x16 9.42 us: add_window(): col_at = send_cols[position]]
  transfers between devices with their start and end apart: 11 -> 9, of which waited for: 9 -> 9; matrix products, arithmetic and copies ran while one was open for 2% -> 0% of each run, Pallas kernels for 0% -> 0%
where the time goes in v1:
time: 223 us
  waiting for transfers between devices  105 us (47%)
  blocking collectives  59.4 us (27%)
  Pallas kernels  21.6 us (10%)
  starting transfers between devices  17.3 us (8%)
  between operations  14.3 us (6%)
  local copies, waits for them, and re-layouts  2.87 us (1%)
  other arithmetic  2.65 us (1%)
    psum x1, waiting for transfers between devices, on_device(): probe_grad = lax.psum(probe_part, ('tile', 'strip', 'mode'))  83.1 us
    all_to_all x1, blocking collectives, on_device(): lax.all_to_all(outgoing, ('tile', 'mode'), split_axis=0, concat_axis=0, t...  30.4 us
    all_to_all x1, blocking collectives, on_device(): lax.all_to_all(back, ('tile', 'mode'), split_axis=0, concat_axis=0, tiled...  29 us
    pallas_call x1, Pallas kernels, on_device(): pl.pallas_call(lambda *refs: position_kernel(n_tile, n_mode, slots, *refs...  9.31 us
    ppermute x2, waiting for transfers between devices, with_halo(): lax.ppermute(lax.slice_in_dim(block, 0, width, axis=dim), axis, backward)  8.84 us
    ppermute x2, waiting for transfers between devices, fold(): high = lax.ppermute(cut(0, width).astype(bf16), axis, backward)  8.73 us
    ppermute x2, starting transfers between devices, with_halo(): lax.ppermute(lax.slice_in_dim(block, block.shape[dim] - width, None, axis...  8.34 us
    pallas_call x1, Pallas kernels, on_device(): pl.pallas_call(lambda *refs: crop_kernel(per_dev, slots, *refs), out_shap...  8.33 us
  transfers between devices with their start and end apart: 9, of which 9 were waited for; matrix products, arithmetic and copies ran while one was open for 0% of the time, Pallas kernels for 0%

profile of v1, /device:TPU:0, one launch (start us, length us, event | category | flops | bytes accessed | tf_op | source)
XLA Modules:
  0.0 223.0 jit_solution(13436391608652124088)
XLA Ops:
  7.2 0.0 copy-start.7
  7.2 0.0 all-reduce.6.cloned.1.call-start
  7.2 1.0 fusion.8
  8.2 4.9 %collective-permute-start = (bf16[2,128,64]{2,1,0:T(8,128)(2,1)S(1)}, bf16[2,128,64]{2,1,0:T(8,128)(2,1)S(1)}, u32[]{:S(2)}, u32[]{:S(2)}) collective-permute-start(bf16[2,128,64]{2,1,0:T(8,128)(2,1)S(1)} %get-tuple-element.16), channel_id=1, source_target_pairs={{0,4},{4,8},{8,12},{1,5},{5,9},{9,13},{2,6},{6,10},{10,14},{3,7},{... | collective-permute-start | bytes 98312 | tf_op jit(solution)/shard_map/ppermute | solution.py:36
  13.2 0.0 copy-start.4
  13.2 0.0 copy-start.5
  13.2 0.0 copy-start.6
  13.2 1.4 collective-permute-start.1
  14.6 0.4 collective-permute-done
  15.0 4.4 %collective-permute-done.1 = bf16[2,128,64]{2,1,0:T(8,128)(2,1)S(1)} collective-permute-done((bf16[2,128,64]{2,1,0:T(8,128)(2,1)S(1)}, bf16[2,128,64]{2,1,0:T(8,128)(2,1)S(1)}, u32[]{:S(2)}, u32[]{:S(2)}) %collective-permute-start.1) | collective-permute-done | bytes 32800 | tf_op jit(solution)/shard_map/ppermute | solution.py:39
  19.5 1.1 pad_maximum_fusion.1
  20.7 3.4 %collective-permute-start.2 = (bf16[2,64,640]{2,1,0:T(8,128)(2,1)S(1)}, bf16[2,64,640]{2,1,0:T(8,128)(2,1)S(1)}, u32[]{:S(2)}, u32[]{:S(2)}) collective-permute-start(bf16[2,64,640]{2,1,0:T(8,128)(2,1)S(1)} %get-tuple-element.14), channel_id=1, source_target_pairs={{0,2},{1,3},{4,6},{5,7},{8,10},{9,11},{12,14},{13,15},{16,18},{17,... | collective-permute-start | bytes 491528 | tf_op jit(solution)/shard_map/ppermute | solution.py:36
  24.1 1.3 collective-permute-start.3
  25.4 1.5 collective-permute-done.2
  26.9 4.4 %collective-permute-done.3 = bf16[2,64,640]{2,1,0:T(8,128)(2,1)S(1)} collective-permute-done((bf16[2,64,640]{2,1,0:T(8,128)(2,1)S(1)}, bf16[2,64,640]{2,1,0:T(8,128)(2,1)S(1)}, u32[]{:S(2)}, u32[]{:S(2)}) %collective-permute-start.3) | collective-permute-done | bytes 163872 | tf_op jit(solution)/shard_map/ppermute | solution.py:39
  31.3 0.0 copy-done.7
  31.3 0.2 pad_maximum_fusion.refs_3_
  31.5 0.0 copy-done.4
  31.5 0.0 copy-done.5
  31.5 0.0 copy-done.6
  31.5 8.3 %crop.1 = bf16[16,2,128,128]{3,2,1,0:T(8,128)(2,1)S(1)} custom-call(s32[32]{0:T(128)S(1)} %bitcast.10, s32[32]{0:T(128)S(1)} %bitcast.13, s32[32]{0:T(128)S(1)} %bitcast.15, bf16[2,256,640]{2,1,0:T(8,128)(2,1)S(1)} %pad_maximum_fusion.refs_3_), custom_call_target="tpu_custom_call" | custom-call | tf_op jit(solution)/shard_map/crop/pallas_call | solution.py:229
  39.9 0.0 copy-start
  39.9 0.0 copy-start.1
  39.9 0.0 copy-start.2
  39.9 0.0 copy-start.3
  39.9 30.4 %all_to_all.10.refs_1_ = bf16[16,2,128,128]{3,2,1,0:T(8,128)(2,1)S(1)} all-to-all(bf16[16,2,128,128]{3,2,1,0:T(8,128)(2,1)S(1)} %crop.1), channel_id=1, replica_groups=mesh['group'=2,'tile'=4,'strip'=2,'mode'=2] {'tile','mode'}, dimensions={0} | all-to-all | bytes 2097152 | tf_op jit(solution)/shard_map/all_to_all | solution.py:237
  70.3 0.0 copy-done
  70.3 0.0 copy-done.1
  70.3 0.0 copy-done.2
  70.3 0.0 copy-done.3
  70.3 9.3 %positions.1 = (bf16[16,2,128,128]{3,2,1,0:T(8,128)(2,1)S(1)}, f32[2,2,128,128]{3,2,1,0:T(8,128)}) custom-call(s32[32]{0:T(128)S(1)} %bitcast.11, bf16[16,2,128,128]{3,2,1,0:T(8,128)(2,1)S(1)} %all_to_all.10.refs_1_, f32[2,2,128,128]{3,2,1,0:T(8,128)S(1)} %copy-done, f32[4,128,128]{2,1,0:T(8,128)S(1)} %bitcast.9, bf16[2,256,256]{2,1,0:T(8,128)(2,1)S(1)} %copy-done.2, ...), custom_call_target="tpu_custom_call" | custom-call | tf_op jit(solution)/shard_map/positions/pallas_call | solution.py:238
  79.6 29.0 %all_to_all.11.refs_3_ = bf16[16,2,128,128]{3,2,1,0:T(8,128)(2,1)S(1)} all-to-all(bf16[16,2,128,128]{3,2,1,0:T(8,128)(2,1)S(1)} %get-tuple-element.4), channel_id=1, replica_groups=mesh['group'=2,'tile'=4,'strip'=2,'mode'=2] {'tile','mode'}, dimensions={0} | all-to-all | bytes 2097152 | tf_op jit(solution)/shard_map/all_to_all | solution.py:247
  108.6 3.9 %scatter.1 = f32[2,256,640]{2,1,0:T(8,128)S(1)} custom-call(s32[32]{0:T(128)S(1)} %bitcast.12, s32[32]{0:T(128)S(1)} %bitcast.14, s32[32]{0:T(128)S(1)} %bitcast.16, bf16[16,2,128,128]{3,2,1,0:T(8,128)(2,1)S(1)} %all_to_all.11.refs_3_), custom_call_target="tpu_custom_call" | custom-call | tf_op jit(solution)/shard_map/scatter/pallas_call | solution.py:248
  112.6 0.1 convert.16
  112.6 0.1 fusion.5
  112.7 2.2 collective-permute-start.4
  115.0 1.3 collective-permute-start.5
  116.3 1.2 collective-permute-done.4
  117.5 4.4 %collective-permute-done.5 = bf16[2,256,64]{2,1,0:T(8,128)(2,1)S(1)} collective-permute-done((bf16[2,256,64]{2,1,0:T(8,128)(2,1)S(1)}, bf16[2,256,64]{2,1,0:T(8,128)(2,1)S(1)}, u32[]{:S(2)}, u32[]{:S(2)}) %collective-permute-start.5) | collective-permute-done | bytes 65568 | tf_op jit(solution)/shard_map/ppermute | solution.py:267
  121.8 0.4 fusion.3
  122.2 1.5 collective-permute-start.6
  123.7 1.3 collective-permute-start.7
  125.0 0.0 all-reduce.6.cloned.1.call-update
  125.0 1.2 collective-permute-done.6
  126.2 4.4 %collective-permute-done.7 = bf16[2,64,512]{2,1,0:T(8,128)(2,1)S(1)} collective-permute-done((bf16[2,64,512]{2,1,0:T(8,128)(2,1)S(1)}, bf16[2,64,512]{2,1,0:T(8,128)(2,1)S(1)}, u32[]{:S(2)}, u32[]{:S(2)}) %collective-permute-start.7) | collective-permute-done | bytes 131104 | tf_op jit(solution)/shard_map/ppermute | solution.py:267
  130.6 0.9 fusion.2
  131.4 83.1 %all-reduce.6.cloned.1.call-done = f32[2,2,128,128]{3,2,1,0:T(8,128)} async-done(((f32[2,2,128,128]{3,2,1,0:T(8,128)}), f32[2,2,128,128]{3,2,1,0:T(8,128)}) %all-reduce.6.cloned.1.call-update) | async-done | bytes 262160 | tf_op jit(solution)/shard_map/psum | solution.py:246
  214.5 1.7 copy.12
  (2 shorter events, 0.1 us)
Async XLA Ops:
  7.2 24.1 %copy-start.7 = (bf16[2,1,128,512]{3,2,1,0:T(8,128)(2,1)S(1)}, bf16[2,1,128,512]{3,2,1,0:T(8,128)(2,1)}, u32[]{:S(2)}) copy-start(bf16[2,1,128,512]{3,2,1,0:T(8,128)(2,1)} %param.8) | copy-start | bytes 786436
  7.2 207.4 %all-reduce.6.cloned.1.call-start = ((), (), s32[]{:S(2)}) async-start(), calls=%async_computation.2 | async-start | bytes 524288 | tf_op jit(solution)/shard_map/psum | solution.py:246
  8.2 6.8 %collective-permute-start = (bf16[2,128,64]{2,1,0:T(8,128)(2,1)S(1)}, bf16[2,128,64]{2,1,0:T(8,128)(2,1)S(1)}, u32[]{:S(2)}, u32[]{:S(2)}) collective-permute-start(bf16[2,128,64]{2,1,0:T(8,128)(2,1)S(1)} %get-tuple-element.16), channel_id=1, source_target_pairs={{0,4},{4,8},{8,12},{1,5},{5,9},{9,13},{2,6},{6,10},{10,14},{3,7},{... | collective-permute-start | bytes 98312 | tf_op jit(solution)/shard_map/ppermute | solution.py:36
  13.2 18.3 %copy-start.4 = (s32[1,32,1]{1,2,0:T(1,128)S(1)}, s32[1,32,1]{1,2,0:T(1,128)}, u32[]{:S(2)}) copy-start(s32[1,32,1]{1,2,0:T(1,128)} %param.11) | copy-start | bytes 388
  13.2 18.3 %copy-start.5 = (s32[1,32]{1,0:T(1,128)S(1)}, s32[1,32]{1,0:T(1,128)}, u32[]{:S(2)}) copy-start(s32[1,32]{1,0:T(1,128)} %param.12) | copy-start | bytes 388
  13.2 18.3 %copy-start.6 = (s32[1,32]{1,0:T(1,128)S(1)}, s32[1,32]{1,0:T(1,128)}, u32[]{:S(2)}) copy-start(s32[1,32]{1,0:T(1,128)} %param.13) | copy-start | bytes 388
  13.2 6.3 %collective-permute-start.1 = (bf16[2,128,64]{2,1,0:T(8,128)(2,1)S(1)}, bf16[2,128,64]{2,1,0:T(8,128)(2,1)S(1)}, u32[]{:S(2)}, u32[]{:S(2)}) collective-permute-start(bf16[2,128,64]{2,1,0:T(8,128)(2,1)S(1)} %get-tuple-element.17), channel_id=1, source_target_pairs={{4,0},{8,4},{12,8},{5,1},{9,5},{13,9},{6,2},{10,6},{14,10},{7,3},{... | collective-permute-start | bytes 98312 | tf_op jit(solution)/shard_map/ppermute | solution.py:39
  20.7 6.2 %collective-permute-start.2 = (bf16[2,64,640]{2,1,0:T(8,128)(2,1)S(1)}, bf16[2,64,640]{2,1,0:T(8,128)(2,1)S(1)}, u32[]{:S(2)}, u32[]{:S(2)}) collective-permute-start(bf16[2,64,640]{2,1,0:T(8,128)(2,1)S(1)} %get-tuple-element.14), channel_id=1, source_target_pairs={{0,2},{1,3},{4,6},{5,7},{8,10},{9,11},{12,14},{13,15},{16,18},{17,... | collective-permute-start | bytes 491528 | tf_op jit(solution)/shard_map/ppermute | solution.py:36
  24.1 7.2 %collective-permute-start.3 = (bf16[2,64,640]{2,1,0:T(8,128)(2,1)S(1)}, bf16[2,64,640]{2,1,0:T(8,128)(2,1)S(1)}, u32[]{:S(2)}, u32[]{:S(2)}) collective-permute-start(bf16[2,64,640]{2,1,0:T(8,128)(2,1)S(1)} %get-tuple-element.15), channel_id=1, source_target_pairs={{2,0},{3,1},{6,4},{7,5},{10,8},{11,9},{14,12},{15,13},{18,16},{19,... | collective-permute-start | bytes 491528 | tf_op jit(solution)/shard_map/ppermute | solution.py:39
  39.9 30.4 %copy-start = (f32[2,2,128,128]{3,2,1,0:T(8,128)S(1)}, f32[2,2,128,128]{3,2,1,0:T(8,128)}, u32[]{:S(2)}) copy-start(f32[2,2,128,128]{3,2,1,0:T(8,128)} %refs_2_.1) | copy-start | bytes 786436
  39.9 30.4 %copy-start.1 = (f32[1,4,128,128]{3,2,1,0:T(8,128)S(1)}, f32[1,4,128,128]{3,2,1,0:T(8,128)}, u32[]{:S(2)}) copy-start(f32[1,4,128,128]{3,2,1,0:T(8,128)} %param.10) | copy-start | bytes 786436
  39.9 30.4 %copy-start.2 = (bf16[2,256,256]{2,1,0:T(8,128)(2,1)S(1)}, bf16[2,256,256]{2,1,0:T(8,128)(2,1)}, u32[]{:S(2)}) copy-start(bf16[2,256,256]{2,1,0:T(8,128)(2,1)} %constant.23.refs_4_) | copy-start | bytes 786436
  39.9 30.4 %copy-start.3 = (f32[2,128,128]{2,1,0:T(8,128)S(1)}, f32[2,128,128]{2,1,0:T(8,128)}, u32[]{:S(2)}) copy-start(f32[2,128,128]{2,1,0:T(8,128)} %constant.9.clone.refs_5_) | copy-start | bytes 393220
  112.7 4.7 %collective-permute-start.4 = (bf16[2,256,64]{2,1,0:T(8,128)(2,1)S(1)}, bf16[2,256,64]{2,1,0:T(8,128)(2,1)S(1)}, u32[]{:S(2)}, u32[]{:S(2)}) collective-permute-start(bf16[2,256,64]{2,1,0:T(8,128)(2,1)S(1)} %get-tuple-element.10), channel_id=1, source_target_pairs={{0,4},{4,8},{8,12},{1,5},{5,9},{9,13},{2,6},{6,10},{10,14},{3,7},{... | collective-permute-start | bytes 196616 | tf_op jit(solution)/shard_map/ppermute | solution.py:266
  115.0 6.9 %collective-permute-start.5 = (bf16[2,256,64]{2,1,0:T(8,128)(2,1)S(1)}, bf16[2,256,64]{2,1,0:T(8,128)(2,1)S(1)}, u32[]{:S(2)}, u32[]{:S(2)}) collective-permute-start(bf16[2,256,64]{2,1,0:T(8,128)(2,1)S(1)} %get-tuple-element.11), channel_id=1, source_target_pairs={{4,0},{8,4},{12,8},{5,1},{9,5},{13,9},{6,2},{10,6},{14,10},{7,3},{... | collective-permute-start | bytes 196616 | tf_op jit(solution)/shard_map/ppermute | solution.py:267
  122.2 4.0 %collective-permute-start.6 = (bf16[2,64,512]{2,1,0:T(8,128)(2,1)S(1)}, bf16[2,64,512]{2,1,0:T(8,128)(2,1)S(1)}, u32[]{:S(2)}, u32[]{:S(2)}) collective-permute-start(bf16[2,64,512]{2,1,0:T(8,128)(2,1)S(1)} %get-tuple-element.12), channel_id=1, source_target_pairs={{0,2},{1,3},{4,6},{5,7},{8,10},{9,11},{12,14},{13,15},{16,18},{17,... | collective-permute-start | bytes 393224 | tf_op jit(solution)/shard_map/ppermute | solution.py:266
  123.7 6.9 %collective-permute-start.7 = (bf16[2,64,512]{2,1,0:T(8,128)(2,1)S(1)}, bf16[2,64,512]{2,1,0:T(8,128)(2,1)S(1)}, u32[]{:S(2)}, u32[]{:S(2)}) collective-permute-start(bf16[2,64,512]{2,1,0:T(8,128)(2,1)S(1)} %get-tuple-element.13), channel_id=1, source_target_pairs={{2,0},{3,1},{6,4},{7,5},{10,8},{11,9},{14,12},{15,13},{18,16},{19,... | collective-permute-start | bytes 393224 | tf_op jit(solution)/shard_map/ppermute | solution.py:267
Sparse Core Ops, SparseCore 0:
  125.1 89.3 all-reduce.5

commit v2 on v1

--- a/solution.py
+++ b/solution.py
@@ -28,19 +28,6 @@
     )
 
 
-def with_halo(block, sides, width):
-    for axis, dim in sides:
-        count = lax.axis_size(axis)
-        forward = [(i, i + 1) for i in range(count - 1)]
-        backward = [(target, source) for source, target in forward]
-        low = lax.ppermute(
-            lax.slice_in_dim(block, block.shape[dim] - width, None, axis=dim), axis, forward
-        )
-        high = lax.ppermute(lax.slice_in_dim(block, 0, width, axis=dim), axis, backward)
-        block = jnp.concatenate([low, block, high], axis=dim)
-    return block
-
-
 def ranks(tile_ref, first, per_dev):
     tiles = [tile_ref[first + q] for q in range(per_dev)]
     out = []
@@ -78,52 +65,292 @@
     return jnp.dot(a, b, preferred_element_type=f32)
 
 
-def column_base(col, width, length):
-    return jnp.minimum(col // length * length, width - 2 * length)
-
-
-def crop_kernel(per_dev, slots, tile_ref, row_ref, col_ref, padded_ref, out_ref):
-    tile = lax.axis_index("tile")
+def remote(src, dst, send, recv, device):
+    return pltpu.make_async_remote_copy(
+        src_ref=src,
+        dst_ref=dst,
+        send_sem=send,
+        recv_sem=recv,
+        device_id=device,
+        device_id_type=pl.DeviceIdType.MESH,
+    )
+
+
+def owner_id(owner, n_mode):
+    return {"tile": owner // n_mode, "mode": owner % n_mode}
+
+
+def others(me, count, act, start=None):
+    first = count // 2 if start is None else start
+
+    def body(step, carry):
+        other = lax.rem(me + first + step, count)
+
+        @pl.when(other != me)
+        def _():
+            act(other)
+
+        return carry
+
+    lax.fori_loop(0, count, body, 0)
+
+
+def greet(me, owners, n_mode, strip, n_strip, neighbours_only):
+    barrier = pltpu.get_barrier_semaphore()
+
+    def call(device):
+        pl.semaphore_signal(barrier, inc=1, device_id=device, device_id_type=pl.DeviceIdType.MESH)
+
+    others(me, owners, lambda other: call(owner_id(other, n_mode)))
+    if neighbours_only:
+        pl.when(strip > 0)(lambda: call({"strip": strip - 1}))
+        pl.when(strip < n_strip - 1)(lambda: call({"strip": strip + 1}))
+        beside = jnp.minimum(strip, 1) + jnp.minimum(n_strip - 1 - strip, 1)
+        pl.semaphore_wait(barrier, owners - 1 + beside)
+    else:
+        others(strip, n_strip, lambda other: call({"strip": other}))
+        pl.semaphore_wait(barrier, owners + n_strip - 2)
+
+
+def swap(axis, here, count, up, down, sends, recvs):
+    to_next = remote(*up, sends.at[0], recvs.at[0], {axis: here + 1})
+    to_prev = remote(*down, sends.at[1], recvs.at[1], {axis: here - 1})
+    has_next, has_prev = here < count - 1, here > 0
+
+    def start():
+        pl.when(has_next)(to_next.start)
+        pl.when(has_prev)(to_prev.start)
+
+    def wait():
+        @pl.when(has_next)
+        def _():
+            to_next.wait_send()
+            remote(*down, sends.at[1], recvs.at[1], {axis: here + 1}).wait_recv()
+
+        @pl.when(has_prev)
+        def _():
+            to_prev.wait_send()
+            remote(*up, sends.at[0], recvs.at[0], {axis: here - 1}).wait_recv()
+
+    return start, wait, has_next, has_prev
+
+
+def forward_kernel(
+    per_dev, slots, n_tile, n_mode, n_strip, margin,
+    tile_ref, row_ref, col_ref, object_ref, arrived_ref,
+    padded_ref, out_ref, tile_send, tile_recv, strip_send, strip_recv, send_sem, recv_sem,
+):
+    tile, mode, strip = (lax.axis_index(axis) for axis in ("tile", "mode", "strip"))
+    me, owners = tile * n_mode + mode, n_tile * n_mode
     length = out_ref.shape[-1]
+    _, tile_rows, tile_cols = object_ref.shape
     _, rows, width = padded_ref.shape
-
-    def body(index, carry):
-        owner, slot = index // slots, index % slots
-        row, col, _ = slot_place((tile_ref, row_ref, col_ref), owner, slot, tile, per_dev)
-        base = column_base(col, width, length)
-        pick_row = one_hot((length, rows), 1, row)
-        pick_col = one_hot((2 * length, length), 0, col - base)
+    own_rows = pl.ds(margin, tile_rows)
+    greet(me, owners, n_mode, strip, n_strip, True)
+    start, wait, has_next, has_prev = swap(
+        "tile", tile, n_tile,
+        (object_ref.at[:, :, pl.ds(tile_cols - length, length)], padded_ref.at[:, own_rows, pl.ds(0, length)]),
+        (object_ref.at[:, :, pl.ds(0, length)], padded_ref.at[:, own_rows, pl.ds(width - length, length)]),
+        tile_send, tile_recv,
+    )
+    start()
+    padded_ref[:, own_rows, pl.ds(length, tile_cols)] = object_ref[...]
+    edge = jnp.zeros((2, tile_rows, length), bf16)
+    flat = jnp.zeros((2, margin, width), bf16)
+
+    @pl.when(jnp.logical_not(has_prev))
+    def _():
+        padded_ref[:, own_rows, pl.ds(0, length)] = edge
+
+    @pl.when(jnp.logical_not(has_next))
+    def _():
+        padded_ref[:, own_rows, pl.ds(width - length, length)] = edge
+
+    wait()
+    start, wait, has_next, has_prev = swap(
+        "strip", strip, n_strip,
+        (padded_ref.at[:, pl.ds(tile_rows, margin), :], padded_ref.at[:, pl.ds(0, margin), :]),
+        (padded_ref.at[:, pl.ds(margin, margin), :], padded_ref.at[:, pl.ds(tile_rows + margin, margin), :]),
+        strip_send, strip_recv,
+    )
+    start()
+
+    @pl.when(jnp.logical_not(has_prev))
+    def _():
+        padded_ref[:, pl.ds(0, margin), :] = flat
+
+    @pl.when(jnp.logical_not(has_next))
+    def _():
+        padded_ref[:, pl.ds(tile_rows + margin, margin), :] = flat
+
+    wait()
+
+    def span(owner):
+        return pl.ds(owner * slots, slots)
+
+    def body(step, carry):
+        owner = lax.rem(me + owners // 2 + step, owners)
+        for slot in range(slots):
+            row, col, _ = slot_place((tile_ref, row_ref, col_ref), owner, slot, tile, per_dev)
+            col = col + margin
+            pick_row = one_hot((length, rows), 1, row)
+            pick_col = one_hot((width, length), 0, col)
+            for part in range(2):
+                window = dot(dot(pick_row, padded_ref[part]).astype(bf16), pick_col)
+                out_ref[owner * slots + slot, part] = window.astype(bf16)
+
+        @pl.when(owner != me)
+        def _():
+            remote(
+                out_ref.at[span(owner)], arrived_ref.at[span(me)],
+                send_sem.at[owner], recv_sem.at[me], owner_id(owner, n_mode),
+            ).start()
+
+        return carry
+
+    lax.fori_loop(0, owners, body, 0)
+    arrived_ref[span(me)] = out_ref[span(me)]
+
+    def finish(other):
+        copy = remote(
+            out_ref.at[span(other)], arrived_ref.at[span(other)],
+            send_sem.at[other], recv_sem.at[other], owner_id(other, n_mode),
+        )
+        copy.wait_send()
+        copy.wait_recv()
+
+    others(me, owners, finish)
+
+
+def backward_kernel(
+    per_dev, slots, n_tile, n_mode, n_strip, margin,
+    tile_ref, row_ref, col_ref, back_ref, part_ref, object_ref, probe_ref,
+    returned_ref, grid_ref, spread_ref, put_ref, rs_ref, sum_ref, strip_ref,
+    col_out, col_in, row_out, row_in,
+    send_sem, recv_sem, rs_send, rs_recv, st_send, st_recv, ag_send, ag_recv,
+    tile_send, tile_recv, strip_send, strip_recv,
+):
+    tile, mode, strip = (lax.axis_index(axis) for axis in ("tile", "mode", "strip"))
+    me, owners = tile * n_mode + mode, n_tile * n_mode
+    count = owners * slots
+    length = back_ref.shape[-1]
+    _, tile_rows, tile_cols = object_ref.shape
+    _, rows, width = grid_ref.shape
+    piece = rs_ref.shape[1]
+    greet(me, owners, n_mode, strip, n_strip, False)
+
+    def span(owner):
+        return pl.ds(owner * slots, slots)
+
+    def share(owner):
+        return pl.ds(pl.multiple_of(owner * piece, piece), piece)
+
+    def reduce_copy(other, source):
+        return remote(
+            part_ref.at[share(other)], rs_ref.at[source],
+            rs_send.at[other], rs_recv.at[source], owner_id(other, n_mode),
+        )
+
+    def window_copy(other, source):
+        return remote(
+            back_ref.at[span(other)], returned_ref.at[span(source)],
+            send_sem.at[other], recv_sem.at[source], owner_id(other, n_mode),
+        )
+
+    def strip_copy(other, source):
+        return remote(
+            sum_ref, strip_ref.at[source], st_send.at[other], st_recv.at[source], {"strip": other}
+        )
+
+    def gather_copy(other, source):
+        return remote(
+            probe_ref.at[share(me)], probe_ref.at[share(source)],
+            ag_send.at[other], ag_recv.at[source], owner_id(other, n_mode),
+        )
+
+    def finish(make):
+        def act(other):
+            make(other, other).wait_send()
+            make(other, other).wait_recv()
+
+        return act
+
+    others(me, owners, lambda other: reduce_copy(other, me).start())
+    others(me, owners, lambda other: window_copy(other, me).start())
+    rs_ref[me] = part_ref[share(me)]
+    returned_ref[span(me)] = back_ref[span(me)]
+    refs = (tile_ref, row_ref, col_ref)
+
+    def build(index, carry):
+        _, col, _ = slot_place(refs, index // slots, index % slots, tile, per_dev)
+        where = pl.ds(pl.multiple_of(index * length, length), length)
+        put_ref[where, :] = one_hot((length, width), 1, col + margin)
+        return carry
+
+    lax.fori_loop(0, count, build, 0)
+    others(me, owners, finish(reduce_copy))
+    sum_ref[...] = lax.fori_loop(1, owners, lambda i, acc: acc + rs_ref[i], rs_ref[0])
+    others(strip, n_strip, lambda other: strip_copy(other, strip).start())
+    strip_ref[strip] = sum_ref[...]
+    others(strip, n_strip, finish(strip_copy))
+    probe_ref[share(me)] = lax.fori_loop(1, n_strip, lambda i, acc: acc + strip_ref[i], strip_ref[0])
+    others(me, owners, lambda other: gather_copy(other, me).start())
+    others(me, owners, finish(window_copy))
+
+    def place(index, carry):
+        row, _, keep = slot_place(refs, index // slots, index % slots, tile, per_dev)
+        where = pl.ds(pl.multiple_of(index * length, length), length)
+        put_row = one_hot((rows, length), 0, row, keep)
         for part in range(2):
-            block = padded_ref[part, :, pl.ds(pl.multiple_of(base, length), 2 * length)]
-            out_ref[index, part] = dot(dot(pick_row, block).astype(bf16), pick_col).astype(bf16)
+            spread_ref[part, :, where] = dot(put_row, returned_ref[index, part]).astype(bf16)
         return carry
 
-    lax.fori_loop(0, out_ref.shape[0], body, 0)
-
-
-def scatter_kernel(per_dev, slots, tile_ref, row_ref, col_ref, back_ref, grid_ref):
-    tile = lax.axis_index("tile")
-    length = back_ref.shape[-1]
-    _, rows, width = grid_ref.shape
-    grid_ref[...] = jnp.zeros_like(grid_ref)
-
-    def body(index, carry):
-        owner, slot = index // slots, index % slots
-        row, col, keep = slot_place((tile_ref, row_ref, col_ref), owner, slot, tile, per_dev)
-        base = column_base(col, width, length)
-
-        @pl.when(keep > 0)
-        def _():
-            put_row = one_hot((rows, length), 0, row)
-            put_col = one_hot((length, 2 * length), 1, col - base)
-            for part in range(2):
-                where = pl.ds(pl.multiple_of(base, length), 2 * length)
-                spread = dot(put_row, back_ref[index, part]).astype(bf16)
-                grid_ref[part, :, where] += dot(spread, put_col)
-
+    lax.fori_loop(0, count, place, 0)
+
+    def fill(block, carry):
+        where = pl.ds(pl.multiple_of(block * 2 * length, 2 * length), 2 * length)
+        for part in range(2):
+            grid_ref[part, :, where] = dot(spread_ref[part], put_ref[:, where])
         return carry
 
-    lax.fori_loop(0, back_ref.shape[0], body, 0)
+    lax.fori_loop(0, width // (2 * length), fill, 0)
+    col_out[0] = grid_ref[:, :, pl.ds(width - length, length)].astype(bf16)
+    col_out[1] = grid_ref[:, :, pl.ds(0, length)].astype(bf16)
+    start, wait, has_next, has_prev = swap(
+        "tile", tile, n_tile,
+        (col_out.at[0], col_in.at[0]), (col_out.at[1], col_in.at[1]), tile_send, tile_recv,
+    )
+    start()
+    wait()
+
+    @pl.when(has_prev)
+    def _():
+        grid_ref[:, :, pl.ds(length, length)] += col_in[0].astype(f32)
+
+    @pl.when(has_next)
+    def _():
+        grid_ref[:, :, pl.ds(width - 2 * length, length)] += col_in[1].astype(f32)
+
+    own = pl.ds(length, tile_cols)
+    row_out[0] = grid_ref[:, pl.ds(margin + tile_rows, margin), own].astype(bf16)
+    row_out[1] = grid_ref[:, pl.ds(0, margin), own].astype(bf16)
+    start, wait, has_next, has_prev = swap(
+        "strip", strip, n_strip,
+        (row_out.at[0], row_in.at[0]), (row_out.at[1], row_in.at[1]), strip_send, strip_recv,
+    )
+    start()
+    object_ref[...] = grid_ref[:, pl.ds(margin, tile_rows), own]
+    wait()
+
+    @pl.when(has_prev)
+    def _():
+        object_ref[:, pl.ds(0, margin), :] += row_in[0].astype(f32)
+
+    @pl.when(has_next)
+    def _():
+        object_ref[:, pl.ds(tile_rows - margin, margin), :] += row_in[1].astype(f32)
+
+    others(me, owners, finish(gather_copy))
 
 
 def split(field, length):
@@ -188,6 +415,7 @@
     owner = lax.axis_index("tile") * n_mode + lax.axis_index("mode")
     tiles, order = ranks(tile_ref, owner * per_dev, per_dev)
     tables = (table_ref[0], table_ref[1])
+    back_ref[...] = jnp.zeros_like(back_ref)
     for q in range(per_dev):
         place = [(tiles[q] * n_mode + k * n_mode // 2) * slots + order[q] for k in range(2)]
         pair = lambda k: (arrived_ref[place[k], 0].astype(f32), arrived_ref[place[k], 1].astype(f32))
@@ -211,6 +439,12 @@
 params = pltpu.CompilerParams(vmem_limit_bytes=vmem_bytes)
 
 
+def communicating(number):
+    return pltpu.CompilerParams(
+        vmem_limit_bytes=vmem_bytes, collective_id=number, has_side_effects=True
+    )
+
+
 def on_device(object_field, probe_modes, measured, pos_tile, off_row, off_col):
     length = probe_modes.shape[-1]
     margin = length // 2
@@ -224,17 +458,25 @@
     count = owners * slots
     tables, prop = make_tables(length)
     places = (pos_tile[0, :, 0], off_row[0], off_col[0])
-    padded = with_halo(object_field[:, 0], (("tile", 2), ("strip", 1)), margin)
+    n_strip = lax.axis_size("strip")
+    sizes = (per_dev, slots, n_tile, n_mode, n_strip, margin)
     windows = jax.ShapeDtypeStruct((count, 2, length, length), bf16)
-    outgoing = pl.pallas_call(
-        lambda *refs: crop_kernel(per_dev, slots, *refs),
+    rows, width = tile_rows + 2 * margin, tile_cols + 2 * length
+    dma = pltpu.SemaphoreType.DMA
+    arrived = pl.pallas_call(
+        lambda *refs: forward_kernel(*sizes, *refs),
         out_shape=windows,
         in_specs=[smem] * 3 + [vmem],
         out_specs=vmem,
-        compiler_params=params,
-        name="crop",
-    )(*places, padded)
-    arrived = lax.all_to_all(outgoing, ("tile", "mode"), split_axis=0, concat_axis=0, tiled=True)
+        scratch_shapes=[
+            pltpu.VMEM((2, rows, width), bf16),
+            pltpu.VMEM(windows.shape, bf16),
+            *[dma((2,))] * 4,
+            *[dma((owners,))] * 2,
+        ],
+        compiler_params=communicating(0),
+        name="forward",
+    )(*places, object_field[:, 0])
     back, probe_part = pl.pallas_call(
         lambda *refs: position_kernel(n_tile, n_mode, slots, *refs),
         out_shape=(windows, jax.ShapeDtypeStruct(probe_modes.shape, f32)),
@@ -243,37 +485,35 @@
         compiler_params=params,
         name="positions",
     )(places[0], arrived, probe_modes, measured[0], tables, prop)
-    probe_grad = lax.psum(probe_part, ("tile", "strip", "mode"))
-    returned = lax.all_to_all(back, ("tile", "mode"), split_axis=0, concat_axis=0, tiled=True)
-    grid = pl.pallas_call(
-        lambda *refs: scatter_kernel(per_dev, slots, *refs),
-        out_shape=jax.ShapeDtypeStruct((2, tile_rows + 2 * margin, tile_cols + 2 * margin), f32),
-        in_specs=[smem] * 3 + [vmem],
-        out_specs=vmem,
-        compiler_params=params,
-        name="scatter",
-    )(*places, returned)
-    folded = fold(grid, "tile", 2, tile_cols, margin)
-    folded = fold(folded, "strip", 1, tile_rows, margin)
-    return (folded[:, None], probe_grad)
-
-
-def fold(grid, axis, dim, count, width):
-    steps = lax.axis_size(axis)
-    forward = [(i, i + 1) for i in range(steps - 1)]
-    backward = [(target, source) for source, target in forward]
-    cut = lambda lo, hi: lax.slice_in_dim(grid, lo, hi, axis=dim)
-    low = lax.ppermute(cut(count + width, count + 2 * width).astype(bf16), axis, forward)
-    high = lax.ppermute(cut(0, width).astype(bf16), axis, backward)
-    low_pad = [(0, 0)] * grid.ndim
-    high_pad = [(0, 0)] * grid.ndim
-    low_pad[dim] = (0, count - width)
-    high_pad[dim] = (count - width, 0)
-    return (
-        cut(width, width + count)
-        + jnp.pad(low.astype(f32), low_pad)
-        + jnp.pad(high.astype(f32), high_pad)
-    )
+    flat = probe_part.reshape(-1, length)
+    piece = flat.shape[0] // owners
+    object_grad, probe_grad = pl.pallas_call(
+        lambda *refs: backward_kernel(*sizes, *refs),
+        out_shape=(
+            jax.ShapeDtypeStruct((2, tile_rows, tile_cols), f32),
+            jax.ShapeDtypeStruct(flat.shape, f32),
+        ),
+        in_specs=[smem] * 3 + [vmem] * 2,
+        out_specs=(vmem, vmem),
+        scratch_shapes=[
+            pltpu.VMEM(windows.shape, bf16),
+            pltpu.VMEM((2, rows, width), f32),
+            pltpu.VMEM((2, rows, count * length), bf16),
+            pltpu.VMEM((count * length, width), bf16),
+            pltpu.VMEM((owners, piece, length), f32),
+            pltpu.VMEM((piece, length), f32),
+            pltpu.VMEM((n_strip, piece, length), f32),
+            *[pltpu.VMEM((2, 2, rows, length), bf16)] * 2,
+            *[pltpu.VMEM((2, 2, margin, tile_cols), bf16)] * 2,
+            *[dma((owners,))] * 4,
+            *[dma((n_strip,))] * 2,
+            *[dma((owners,))] * 2,
+            *[dma((2,))] * 4,
+        ],
+        compiler_params=communicating(1),
+        name="backward",
+    )(*places, back, flat)
+    return (object_grad[:, None], probe_grad.reshape(probe_modes.shape))
 
 
 def solution(mesh):

time: 223 us -> 102 us (0.46)
  waiting for transfers between devices: 105 us -> 0 us
  Pallas kernels: 21.6 us -> 98 us
  blocking collectives: 59.4 us -> 0 us
  starting transfers between devices: 17.3 us -> 0 us
  between operations: 14.3 us -> 0.72 us
  other arithmetic: 2.65 us -> 0 us
    psum x1 -> x0, waiting for transfers between devices: 83.1 us -> none  [on_device(): probe_grad = lax.psum(probe_part, ('tile', 'strip', 'mode'))]
    pallas_call x2, Pallas kernels: 12.2 us -> 89.4 us  [the longest x1 49.8 us: on_device(): pl.pallas_call(lambda *refs: backward_kernel(*sizes, *refs), out_shape=(j...]
    all_to_all x2 -> x0, blocking collectives: 59.4 us -> none  [the longest x1 30.4 us: on_device(): lax.all_to_all(outgoing, ('tile', 'mode'), split_axis=0, concat_axis=0, t...]
    ppermute x8 -> x0, waiting for transfers between devices: 21.9 us -> none  [the longest x2 8.84 us: with_halo(): lax.ppermute(lax.slice_in_dim(block, 0, width, axis=dim), axis, backward)]
    ppermute x8 -> x0, starting transfers between devices: 17.3 us -> none  [the longest x2 8.34 us: with_halo(): lax.ppermute(lax.slice_in_dim(block, block.shape[dim] - width, None, axis...]
  transfers between devices with their start and end apart: 9 -> 0, of which waited for: 9 -> 0; matrix products, arithmetic and copies ran while one was open for 0% -> 0% of each run, Pallas kernels for 0% -> 0%
where the time goes in v2:
time: 102 us
  Pallas kernels  98 us (96%)
  local copies, waits for them, and re-layouts  3.13 us (3%)
    pallas_call x1, Pallas kernels, on_device(): pl.pallas_call(lambda *refs: backward_kernel(*sizes, *refs), out_shape=(j...  49.8 us
    pallas_call x1, Pallas kernels, on_device(): pl.pallas_call(lambda *refs: forward_kernel(*sizes, *refs), out_shape=win...  39.6 us
    pallas_call x1, Pallas kernels, on_device(): pl.pallas_call(lambda *refs: position_kernel(n_tile, n_mode, slots, *refs...  8.68 us
    unnamed x18, local copies, waits for them, and re-layouts  3.13 us

profile of v2, /device:TPU:0, one launch (start us, length us, event | category | flops | bytes accessed | tf_op | source)
XLA Modules:
  0.0 101.9 jit_solution(6451496814307674612)
XLA Ops:
  0.6 0.0 copy-start.5
  0.6 0.0 copy-start.6
  0.7 0.0 copy-start.7
  0.7 0.6 copy-done.5
  1.3 0.0 copy-done.6
  1.3 0.0 copy-done.7
  1.3 0.0 copy-start.3
  1.3 0.9 copy-done.3
  2.3 0.0 copy-start
  2.3 0.0 copy-start.1
  2.3 0.0 copy-start.2
  2.3 0.0 copy-start.4
  2.3 39.6 %forward.1.refs_1_ = bf16[16,2,128,128]{3,2,1,0:T(8,128)(2,1)S(1)} custom-call(s32[32]{0:T(128)S(1)} %bitcast.15, s32[32]{0:T(128)S(1)} %bitcast.18, s32[32]{0:T(128)S(1)} %bitcast.20, bf16[2,128,512]{2,1,0:T(8,128)(2,1)S(1)} %bitcast.13), custom_call_target="tpu_custom_call" | custom-call | tf_op jit(solution)/shard_map/forward/pallas_call | solution.py:466
  41.9 0.0 copy-done
  41.9 0.0 copy-done.1
  41.9 0.0 copy-done.2
  41.9 0.0 copy-done.4
  41.9 8.7 %positions.1 = (bf16[16,2,128,128]{3,2,1,0:T(8,128)(2,1)S(1)}, f32[2,2,128,128]{3,2,1,0:T(8,128)S(1)}) custom-call(s32[32]{0:T(128)S(1)} %bitcast.16, bf16[16,2,128,128]{3,2,1,0:T(8,128)(2,1)S(1)} %forward.1.refs_1_, f32[2,2,128,128]{3,2,1,0:T(8,128)S(1)} %copy-done, f32[4,128,128]{2,1,0:T(8,128)S(1)} %bitcast.11, bf16[2,256,256]{2,1,0:T(8,128)(2,1)S(1)} %copy-done.2, ...), custom_call_target="tpu_custom_call" | custom-call | tf_op jit(solution)/shard_map/positions/pallas_call | solution.py:480
  50.6 49.8 %backward.1 = (f32[2,128,512]{2,1,0:T(8,128)S(1)}, f32[512,128]{1,0:T(8,128)S(1)}) custom-call(s32[32]{0:T(128)S(1)} %bitcast.17, s32[32]{0:T(128)S(1)} %bitcast.19, s32[32]{0:T(128)S(1)} %bitcast.21, bf16[16,2,128,128]{3,2,1,0:T(8,128)(2,1)S(1)} %get-tuple-element.6.refs_3_, f32[512,128]{1,0:T(8,128)S(1)} %bitcast.14), custom_call_target="tpu_custom_call" | custom-call | tf_op jit(solution)/shard_map/backward/pallas_call | solution.py:490
  100.4 0.8 copy.13
  101.2 0.7 copy.14
Async XLA Ops:
  0.6 0.7 copy-start.5
  0.6 0.7 copy-start.6
  0.7 0.7 copy-start.7
  1.3 0.9 copy-start.3
  2.3 39.6 %copy-start = (f32[2,2,128,128]{3,2,1,0:T(8,128)S(1)}, f32[2,2,128,128]{3,2,1,0:T(8,128)}, u32[]{:S(2)}) copy-start(f32[2,2,128,128]{3,2,1,0:T(8,128)} %refs_2_.1) | copy-start | bytes 786436
  2.3 39.6 %copy-start.1 = (f32[1,4,128,128]{3,2,1,0:T(8,128)S(1)}, f32[1,4,128,128]{3,2,1,0:T(8,128)}, u32[]{:S(2)}) copy-start(f32[1,4,128,128]{3,2,1,0:T(8,128)} %param.10) | copy-start | bytes 786436
  2.3 39.6 %copy-start.2 = (bf16[2,256,256]{2,1,0:T(8,128)(2,1)S(1)}, bf16[2,256,256]{2,1,0:T(8,128)(2,1)}, u32[]{:S(2)}) copy-start(bf16[2,256,256]{2,1,0:T(8,128)(2,1)} %constant.11.refs_4_) | copy-start | bytes 786436
  2.3 39.6 %copy-start.4 = (f32[2,128,128]{2,1,0:T(8,128)S(1)}, f32[2,128,128]{2,1,0:T(8,128)}, u32[]{:S(2)}) copy-start(f32[2,128,128]{2,1,0:T(8,128)} %constant.5.clone.refs_5_) | copy-start | bytes 393220

commit v3 on v2

--- a/solution.py
+++ b/solution.py
@@ -95,95 +95,96 @@
     lax.fori_loop(0, count, body, 0)
 
 
-def greet(me, owners, n_mode, strip, n_strip, neighbours_only):
+directions = [(dt, ds) for ds in (-1, 0, 1) for dt in (-1, 0, 1) if (dt, ds) != (0, 0)]
+
+
+def exists(here, count, step):
+    if step == 0:
+        return jnp.int32(1)
+    return jnp.minimum(count - 1 - here if step > 0 else here, 1)
+
+
+def neighbour(spot, direction, sign):
+    tile, strip, n_tile, n_strip = spot
+    dt, ds = (sign * d for d in direction)
+    there = exists(tile, n_tile, dt) * exists(strip, n_strip, ds)
+    return there, {"tile": tile + dt, "strip": strip + ds}
+
+
+def greet(me, owners, n_mode, spot):
     barrier = pltpu.get_barrier_semaphore()
+    tile, strip, n_tile, n_strip = spot
 
     def call(device):
         pl.semaphore_signal(barrier, inc=1, device_id=device, device_id_type=pl.DeviceIdType.MESH)
 
     others(me, owners, lambda other: call(owner_id(other, n_mode)))
-    if neighbours_only:
-        pl.when(strip > 0)(lambda: call({"strip": strip - 1}))
-        pl.when(strip < n_strip - 1)(lambda: call({"strip": strip + 1}))
-        beside = jnp.minimum(strip, 1) + jnp.minimum(n_strip - 1 - strip, 1)
-        pl.semaphore_wait(barrier, owners - 1 + beside)
-    else:
-        others(strip, n_strip, lambda other: call({"strip": other}))
-        pl.semaphore_wait(barrier, owners + n_strip - 2)
-
-
-def swap(axis, here, count, up, down, sends, recvs):
-    to_next = remote(*up, sends.at[0], recvs.at[0], {axis: here + 1})
-    to_prev = remote(*down, sends.at[1], recvs.at[1], {axis: here - 1})
-    has_next, has_prev = here < count - 1, here > 0
-
-    def start():
-        pl.when(has_next)(to_next.start)
-        pl.when(has_prev)(to_prev.start)
-
-    def wait():
-        @pl.when(has_next)
-        def _():
-            to_next.wait_send()
-            remote(*down, sends.at[1], recvs.at[1], {axis: here + 1}).wait_recv()
-
-        @pl.when(has_prev)
-        def _():
-            to_prev.wait_send()
-            remote(*up, sends.at[0], recvs.at[0], {axis: here - 1}).wait_recv()
-
-    return start, wait, has_next, has_prev
+    others(strip, n_strip, lambda other: call({"strip": other}))
+    amount = owners + n_strip - 2
+    for direction in directions:
+        if 0 not in direction:
+            there, device = neighbour(spot, direction, 1)
+            pl.when(there > 0)(lambda: call(device))
+            amount = amount + there
+    pl.semaphore_wait(barrier, amount)
+
+
+def side(step, before, middle, after):
+    return ((0, before), (before, middle), (before + middle, after))[step + 1]
+
+
+def margin_part(ref, dt, ds, tile_rows, tile_cols, margin, length):
+    row, row_count = side(ds, margin, tile_rows, margin)
+    col, col_count = side(dt, length, tile_cols, length)
+    return ref.at[:, pl.ds(row, row_count), pl.ds(col, col_count)]
 
 
 def forward_kernel(
     per_dev, slots, n_tile, n_mode, n_strip, margin,
     tile_ref, row_ref, col_ref, object_ref, arrived_ref,
-    padded_ref, out_ref, tile_send, tile_recv, strip_send, strip_recv, send_sem, recv_sem,
+    padded_ref, out_ref, halo_send, halo_recv, send_sem, recv_sem,
 ):
     tile, mode, strip = (lax.axis_index(axis) for axis in ("tile", "mode", "strip"))
     me, owners = tile * n_mode + mode, n_tile * n_mode
     length = out_ref.shape[-1]
     _, tile_rows, tile_cols = object_ref.shape
     _, rows, width = padded_ref.shape
-    own_rows = pl.ds(margin, tile_rows)
-    greet(me, owners, n_mode, strip, n_strip, True)
-    start, wait, has_next, has_prev = swap(
-        "tile", tile, n_tile,
-        (object_ref.at[:, :, pl.ds(tile_cols - length, length)], padded_ref.at[:, own_rows, pl.ds(0, length)]),
-        (object_ref.at[:, :, pl.ds(0, length)], padded_ref.at[:, own_rows, pl.ds(width - length, length)]),
-        tile_send, tile_recv,
-    )
-    start()
-    padded_ref[:, own_rows, pl.ds(length, tile_cols)] = object_ref[...]
-    edge = jnp.zeros((2, tile_rows, length), bf16)
-    flat = jnp.zeros((2, margin, width), bf16)
-
-    @pl.when(jnp.logical_not(has_prev))
-    def _():
-        padded_ref[:, own_rows, pl.ds(0, length)] = edge
-
-    @pl.when(jnp.logical_not(has_next))
-    def _():
-        padded_ref[:, own_rows, pl.ds(width - length, length)] = edge
-
-    wait()
-    start, wait, has_next, has_prev = swap(
-        "strip", strip, n_strip,
-        (padded_ref.at[:, pl.ds(tile_rows, margin), :], padded_ref.at[:, pl.ds(0, margin), :]),
-        (padded_ref.at[:, pl.ds(margin, margin), :], padded_ref.at[:, pl.ds(tile_rows + margin, margin), :]),
-        strip_send, strip_recv,
-    )
-    start()
-
-    @pl.when(jnp.logical_not(has_prev))
-    def _():
-        padded_ref[:, pl.ds(0, margin), :] = flat
-
-    @pl.when(jnp.logical_not(has_next))
-    def _():
-        padded_ref[:, pl.ds(tile_rows + margin, margin), :] = flat
-
-    wait()
+    spot = (tile, strip, n_tile, n_strip)
+    greet(me, owners, n_mode, spot)
+
+    def edge(dt, ds):
+        row = {1: tile_rows - margin}.get(ds, 0)
+        col = {1: tile_cols - length}.get(dt, 0)
+        return object_ref.at[
+            :, pl.ds(row, margin if ds else tile_rows), pl.ds(col, length if dt else tile_cols)
+        ]
+
+    def region(dt, ds):
+        return margin_part(padded_ref, dt, ds, tile_rows, tile_cols, margin, length)
+
+    def halo(number, sign):
+        dt, ds = directions[number]
+        there, device = neighbour(spot, (dt, ds), sign)
+        copy = remote(edge(dt, ds), region(-dt, -ds), halo_send.at[number], halo_recv.at[number], device)
+        return there, copy
+
+    for number in range(len(directions)):
+        there, copy = halo(number, 1)
+        pl.when(there > 0)(copy.start)
+    region(0, 0)[...] = object_ref[...]
+    for number, (dt, ds) in enumerate(directions):
+        there, _ = neighbour(spot, (dt, ds), -1)
+        target = region(-dt, -ds)
+
+        @pl.when(there == 0)
+        def _():
+            target[...] = jnp.zeros(target.shape, bf16)
+
+    for number in range(len(directions)):
+        there, copy = halo(number, 1)
+        pl.when(there > 0)(copy.wait_send)
+        there, copy = halo(number, -1)
+        pl.when(there > 0)(copy.wait_recv)
 
     def span(owner):
         return pl.ds(owner * slots, slots)
@@ -225,10 +226,10 @@
 def backward_kernel(
     per_dev, slots, n_tile, n_mode, n_strip, margin,
     tile_ref, row_ref, col_ref, back_ref, part_ref, object_ref, probe_ref,
-    returned_ref, grid_ref, spread_ref, put_ref, rs_ref, sum_ref, strip_ref,
-    col_out, col_in, row_out, row_in,
-    send_sem, recv_sem, rs_send, rs_recv, st_send, st_recv, ag_send, ag_recv,
-    tile_send, tile_recv, strip_send, strip_recv,
+    returned_ref, grid_ref, spread_ref, put_ref, pair_ref, half_ref, rs_ref, sum_ref, strip_ref,
+    margin_out, margin_in,
+    send_sem, recv_sem, pair_send, pair_recv, rs_send, rs_recv, st_send, st_recv,
+    ag_send, ag_recv, join_send, join_recv, margin_send, margin_recv,
 ):
     tile, mode, strip = (lax.axis_index(axis) for axis in ("tile", "mode", "strip"))
     me, owners = tile * n_mode + mode, n_tile * n_mode
@@ -237,18 +238,26 @@
     _, tile_rows, tile_cols = object_ref.shape
     _, rows, width = grid_ref.shape
     piece = rs_ref.shape[1]
-    greet(me, owners, n_mode, strip, n_strip, False)
+    half = n_tile * piece
+    spot = (tile, strip, n_tile, n_strip)
+    greet(me, owners, n_mode, spot)
 
     def span(owner):
         return pl.ds(owner * slots, slots)
 
-    def share(owner):
-        return pl.ds(pl.multiple_of(owner * piece, piece), piece)
+    def share(index, size):
+        return pl.ds(pl.multiple_of(index * size, piece), size)
+
+    def pair_copy(other, source):
+        return remote(
+            part_ref.at[share(other, half)], pair_ref.at[source],
+            pair_send.at[other], pair_recv.at[source], {"mode": other},
+        )
 
     def reduce_copy(other, source):
         return remote(
-            part_ref.at[share(other)], rs_ref.at[source],
-            rs_send.at[other], rs_recv.at[source], owner_id(other, n_mode),
+            half_ref.at[share(other, piece)], rs_ref.at[source],
+            rs_send.at[other], rs_recv.at[source], {"tile": other},
         )
 
     def window_copy(other, source):
@@ -264,8 +273,15 @@
 
     def gather_copy(other, source):
         return remote(
-            probe_ref.at[share(me)], probe_ref.at[share(source)],
-            ag_send.at[other], ag_recv.at[source], owner_id(other, n_mode),
+            probe_ref.at[share(mode * n_tile + tile, piece)],
+            probe_ref.at[share(mode * n_tile + source, piece)],
+            ag_send.at[other], ag_recv.at[source], {"tile": other},
+        )
+
+    def join_copy(other, source):
+        return remote(
+            probe_ref.at[share(mode, half)], probe_ref.at[share(source, half)],
+            join_send.at[other], join_recv.at[source], {"mode": other},
         )
 
     def finish(make):
@@ -275,10 +291,14 @@
 
         return act
 
-    others(me, owners, lambda other: reduce_copy(other, me).start())
+    others(mode, n_mode, lambda other: pair_copy(other, mode).start())
     others(me, owners, lambda other: window_copy(other, me).start())
-    rs_ref[me] = part_ref[share(me)]
+    pair_ref[mode] = part_ref[share(mode, half)]
     returned_ref[span(me)] = back_ref[span(me)]
+    others(mode, n_mode, finish(pair_copy))
+    half_ref[...] = lax.fori_loop(1, n_mode, lambda i, acc: acc + pair_ref[i], pair_ref[0])
+    others(tile, n_tile, lambda other: reduce_copy(other, tile).start())
+    rs_ref[tile] = half_ref[share(tile, piece)]
     refs = (tile_ref, row_ref, col_ref)
 
     def build(index, carry):
@@ -288,69 +308,83 @@
         return carry
 
     lax.fori_loop(0, count, build, 0)
-    others(me, owners, finish(reduce_copy))
-    sum_ref[...] = lax.fori_loop(1, owners, lambda i, acc: acc + rs_ref[i], rs_ref[0])
+    others(tile, n_tile, finish(reduce_copy))
+    sum_ref[...] = lax.fori_loop(1, n_tile, lambda i, acc: acc + rs_ref[i], rs_ref[0])
     others(strip, n_strip, lambda other: strip_copy(other, strip).start())
     strip_ref[strip] = sum_ref[...]
     others(strip, n_strip, finish(strip_copy))
-    probe_ref[share(me)] = lax.fori_loop(1, n_strip, lambda i, acc: acc + strip_ref[i], strip_ref[0])
-    others(me, owners, lambda other: gather_copy(other, me).start())
-    others(me, owners, finish(window_copy))
-
-    def place(index, carry):
-        row, _, keep = slot_place(refs, index // slots, index % slots, tile, per_dev)
-        where = pl.ds(pl.multiple_of(index * length, length), length)
-        put_row = one_hot((rows, length), 0, row, keep)
-        for part in range(2):
-            spread_ref[part, :, where] = dot(put_row, returned_ref[index, part]).astype(bf16)
+    probe_ref[share(mode * n_tile + tile, piece)] = lax.fori_loop(
+        1, n_strip, lambda i, acc: acc + strip_ref[i], strip_ref[0]
+    )
+    others(tile, n_tile, lambda other: gather_copy(other, tile).start())
+
+    def place(step, carry):
+        owner = lax.rem(me + 2 * owners - owners // 2 - step, owners)
+
+        @pl.when(owner != me)
+        def _():
+            finish(window_copy)(owner)
+
+        for slot in range(slots):
+            index = owner * slots + slot
+            row, _, keep = slot_place(refs, owner, slot, tile, per_dev)
+            where = pl.ds(pl.multiple_of(index * length, length), length)
+            put_row = one_hot((rows, length), 0, row, keep)
+            for part in range(2):
+                spread_ref[part, :, where] = dot(put_row, returned_ref[index, part]).astype(bf16)
         return carry
 
-    lax.fori_loop(0, count, place, 0)
-
-    def fill(block, carry):
-        where = pl.ds(pl.multiple_of(block * 2 * length, 2 * length), 2 * length)
+    lax.fori_loop(0, owners, place, 0)
+
+    def fill(col, size):
+        where = pl.ds(col, size)
         for part in range(2):
             grid_ref[part, :, where] = dot(spread_ref[part], put_ref[:, where])
-        return carry
-
-    lax.fori_loop(0, width // (2 * length), fill, 0)
-    col_out[0] = grid_ref[:, :, pl.ds(width - length, length)].astype(bf16)
-    col_out[1] = grid_ref[:, :, pl.ds(0, length)].astype(bf16)
-    start, wait, has_next, has_prev = swap(
-        "tile", tile, n_tile,
-        (col_out.at[0], col_in.at[0]), (col_out.at[1], col_in.at[1]), tile_send, tile_recv,
-    )
-    start()
-    wait()
-
-    @pl.when(has_prev)
-    def _():
-        grid_ref[:, :, pl.ds(length, length)] += col_in[0].astype(f32)
-
-    @pl.when(has_next)
-    def _():
-        grid_ref[:, :, pl.ds(width - 2 * length, length)] += col_in[1].astype(f32)
-
-    own = pl.ds(length, tile_cols)
-    row_out[0] = grid_ref[:, pl.ds(margin + tile_rows, margin), own].astype(bf16)
-    row_out[1] = grid_ref[:, pl.ds(0, margin), own].astype(bf16)
-    start, wait, has_next, has_prev = swap(
-        "strip", strip, n_strip,
-        (row_out.at[0], row_in.at[0]), (row_out.at[1], row_in.at[1]), strip_send, strip_recv,
-    )
-    start()
-    object_ref[...] = grid_ref[:, pl.ds(margin, tile_rows), own]
-    wait()
-
-    @pl.when(has_prev)
-    def _():
-        object_ref[:, pl.ds(0, margin), :] += row_in[0].astype(f32)
-
-    @pl.when(has_next)
-    def _():
-        object_ref[:, pl.ds(tile_rows - margin, margin), :] += row_in[1].astype(f32)
-
-    others(me, owners, finish(gather_copy))
+
+    def region(ref, dt, ds):
+        return margin_part(ref, dt, ds, tile_rows, tile_cols, margin, length)
+
+    def margin_copy(number, sign):
+        dt, ds = directions[number]
+        there, device = neighbour(spot, (dt, ds), sign)
+        copy = remote(
+            region(margin_out, dt, ds), region(margin_in, -dt, -ds),
+            margin_send.at[number], margin_recv.at[number], device,
+        )
+        return there, copy
+
+    def send_margins(columns):
+        for number, (dt, ds) in enumerate(directions):
+            if (dt != 0) == columns:
+                region(margin_out, dt, ds)[...] = region(grid_ref, dt, ds)[...].astype(bf16)
+                there, copy = margin_copy(number, 1)
+                pl.when(there > 0)(copy.start)
+
+    fill(0, 2 * length)
+    fill(width - 2 * length, 2 * length)
+    send_margins(True)
+    fill(2 * length, width - 4 * length)
+    send_margins(False)
+    others(tile, n_tile, finish(gather_copy))
+    others(mode, n_mode, lambda other: join_copy(other, mode).start())
+    object_ref[...] = region(grid_ref, 0, 0)[...]
+    for number, (dt, ds) in enumerate(directions):
+        there, copy = margin_copy(number, 1)
+        pl.when(there > 0)(copy.wait_send)
+        there, copy = margin_copy(number, -1)
+        row = {-1: tile_rows - margin}.get(ds, 0)
+        col = {-1: tile_cols - length}.get(dt, 0)
+        target = object_ref.at[
+            :, pl.ds(row, margin if ds else tile_rows), pl.ds(col, length if dt else tile_cols)
+        ]
+        arriving = region(margin_in, -dt, -ds)
+
+        @pl.when(there > 0)
+        def _():
+            copy.wait_recv()
+            target[...] += arriving[...].astype(f32)
+
+    others(mode, n_mode, finish(join_copy))
 
 
 def split(field, length):
@@ -471,7 +505,7 @@
         scratch_shapes=[
             pltpu.VMEM((2, rows, width), bf16),
             pltpu.VMEM(windows.shape, bf16),
-            *[dma((2,))] * 4,
+            *[dma((len(directions),))] * 2,
             *[dma((owners,))] * 2,
         ],
         compiler_params=communicating(0),
@@ -500,15 +534,19 @@
             pltpu.VMEM((2, rows, width), f32),
             pltpu.VMEM((2, rows, count * length), bf16),
             pltpu.VMEM((count * length, width), bf16),
-            pltpu.VMEM((owners, piece, length), f32),
+            pltpu.VMEM((n_mode, n_tile * piece, length), f32),
+            pltpu.VMEM((n_tile * piece, length), f32),
+            pltpu.VMEM((n_tile, piece, length), f32),
             pltpu.VMEM((piece, length), f32),
             pltpu.VMEM((n_strip, piece, length), f32),
-            *[pltpu.VMEM((2, 2, rows, length), bf16)] * 2,
-            *[pltpu.VMEM((2, 2, margin, tile_cols), bf16)] * 2,
-            *[dma((owners,))] * 4,
+            *[pltpu.VMEM((2, rows, width), bf16)] * 2,
+            *[dma((owners,))] * 2,
+            *[dma((n_mode,))] * 2,
+            *[dma((n_tile,))] * 2,
             *[dma((n_strip,))] * 2,
-            *[dma((owners,))] * 2,
-            *[dma((2,))] * 4,
+            *[dma((n_tile,))] * 2,
+            *[dma((n_mode,))] * 2,
+            *[dma((len(directions),))] * 2,
         ],
         compiler_params=communicating(1),
         name="backward",

time: 102 us -> 90.8 us (0.89)
  Pallas kernels: 98 us -> 86.8 us
    pallas_call x1, Pallas kernels: 49.8 us -> 42 us  [on_device(): pl.pallas_call(lambda *refs: backward_kernel(*sizes, *refs), out_shape=(j...]
    pallas_call x1, Pallas kernels: 39.6 us -> 36.2 us  [on_device(): pl.pallas_call(lambda *refs: forward_kernel(*sizes, *refs), out_shape=win...]
where the time goes in v3:
time: 90.8 us; the launch traced here: 90.7 us
  Pallas kernels  86.8 us (96%)
  local copies, waits for them, and re-layouts  3.13 us (3%)
    pallas_call x1, Pallas kernels, on_device(): pl.pallas_call(lambda *refs: backward_kernel(*sizes, *refs), out_shape=(j...  42 us
    pallas_call x1, Pallas kernels, on_device(): pl.pallas_call(lambda *refs: forward_kernel(*sizes, *refs), out_shape=win...  36.2 us
    pallas_call x1, Pallas kernels, on_device(): pl.pallas_call(lambda *refs: position_kernel(n_tile, n_mode, slots, *refs...  8.67 us
    unnamed x18, local copies, waits for them, and re-layouts  3.13 us

profile of v3, /device:TPU:0, one launch (start us, length us, event | category | flops | bytes accessed | tf_op | source)
XLA Modules:
  0.0 90.7 jit_solution(10197007100327142412)
XLA Ops:
  0.6 0.0 copy-start.5
  0.6 0.0 copy-start.6
  0.7 0.0 copy-start.7
  0.7 0.6 copy-done.5
  1.3 0.0 copy-done.6
  1.3 0.0 copy-done.7
  1.3 0.0 copy-start.3
  1.3 0.9 %copy-done.3 = bf16[2,1,128,512]{3,2,1,0:T(8,128)(2,1)S(1)} copy-done((bf16[2,1,128,512]{3,2,1,0:T(8,128)(2,1)S(1)}, bf16[2,1,128,512]{3,2,1,0:T(8,128)(2,1)}, u32[]{:S(2)}) %copy-start.3) | copy-done | bytes 262168
  2.3 0.0 copy-start
  2.3 0.0 copy-start.1
  2.3 0.0 copy-start.2
  2.3 0.0 copy-start.4
  2.3 36.2 %forward.1.refs_1_ = bf16[16,2,128,128]{3,2,1,0:T(8,128)(2,1)S(1)} custom-call(s32[32]{0:T(128)S(1)} %bitcast.15, s32[32]{0:T(128)S(1)} %bitcast.18, s32[32]{0:T(128)S(1)} %bitcast.20, bf16[2,128,512]{2,1,0:T(8,128)(2,1)S(1)} %bitcast.13), custom_call_target="tpu_custom_call" | custom-call | tf_op jit(solution)/shard_map/forward/pallas_call | solution.py:500
  38.4 0.0 copy-done
  38.5 0.0 copy-done.1
  38.5 0.0 copy-done.2
  38.5 0.0 copy-done.4
  38.5 8.7 %positions.1 = (bf16[16,2,128,128]{3,2,1,0:T(8,128)(2,1)S(1)}, f32[2,2,128,128]{3,2,1,0:T(8,128)S(1)}) custom-call(s32[32]{0:T(128)S(1)} %bitcast.16, bf16[16,2,128,128]{3,2,1,0:T(8,128)(2,1)S(1)} %forward.1.refs_1_, f32[2,2,128,128]{3,2,1,0:T(8,128)S(1)} %copy-done, f32[4,128,128]{2,1,0:T(8,128)S(1)} %bitcast.11, bf16[2,256,256]{2,1,0:T(8,128)(2,1)S(1)} %copy-done.2, ...), custom_call_target="tpu_custom_call" | custom-call | tf_op jit(solution)/shard_map/positions/pallas_call | solution.py:514
  47.2 42.0 %backward.1 = (f32[2,128,512]{2,1,0:T(8,128)S(1)}, f32[512,128]{1,0:T(8,128)S(1)}) custom-call(s32[32]{0:T(128)S(1)} %bitcast.17, s32[32]{0:T(128)S(1)} %bitcast.19, s32[32]{0:T(128)S(1)} %bitcast.21, bf16[16,2,128,128]{3,2,1,0:T(8,128)(2,1)S(1)} %get-tuple-element.6.refs_3_, f32[512,128]{1,0:T(8,128)S(1)} %bitcast.14), custom_call_target="tpu_custom_call" | custom-call | tf_op jit(solution)/shard_map/backward/pallas_call | solution.py:524
  89.2 0.8 copy.13
  90.0 0.7 copy.14
Async XLA Ops:
  0.6 0.7 copy-start.5
  0.6 0.7 copy-start.6
  0.7 0.7 copy-start.7
  1.3 0.9 %copy-start.3 = (bf16[2,1,128,512]{3,2,1,0:T(8,128)(2,1)S(1)}, bf16[2,1,128,512]{3,2,1,0:T(8,128)(2,1)}, u32[]{:S(2)}) copy-start(bf16[2,1,128,512]{3,2,1,0:T(8,128)(2,1)} %param.8) | copy-start | bytes 786436
  2.3 36.2 %copy-start = (f32[2,2,128,128]{3,2,1,0:T(8,128)S(1)}, f32[2,2,128,128]{3,2,1,0:T(8,128)}, u32[]{:S(2)}) copy-start(f32[2,2,128,128]{3,2,1,0:T(8,128)} %refs_2_.1) | copy-start | bytes 786436
  2.3 36.2 %copy-start.1 = (f32[1,4,128,128]{3,2,1,0:T(8,128)S(1)}, f32[1,4,128,128]{3,2,1,0:T(8,128)}, u32[]{:S(2)}) copy-start(f32[1,4,128,128]{3,2,1,0:T(8,128)} %param.10) | copy-start | bytes 786436
  2.3 36.2 %copy-start.2 = (bf16[2,256,256]{2,1,0:T(8,128)(2,1)S(1)}, bf16[2,256,256]{2,1,0:T(8,128)(2,1)}, u32[]{:S(2)}) copy-start(bf16[2,256,256]{2,1,0:T(8,128)(2,1)} %constant.11.refs_4_) | copy-start | bytes 786436
  2.3 36.2 %copy-start.4 = (f32[2,128,128]{2,1,0:T(8,128)S(1)}, f32[2,128,128]{2,1,0:T(8,128)}, u32[]{:S(2)}) copy-start(f32[2,128,128]{2,1,0:T(8,128)} %constant.5.clone.refs_5_) | copy-start | bytes 393220

commit v4 on v3

--- a/solution.py
+++ b/solution.py
@@ -195,9 +195,14 @@
             row, col, _ = slot_place((tile_ref, row_ref, col_ref), owner, slot, tile, per_dev)
             col = col + margin
             pick_row = one_hot((length, rows), 1, row)
-            pick_col = one_hot((width, length), 0, col)
+            outer = 2 * length
+            pick_col = one_hot((2 * outer, length), 0, jnp.where(col < outer, col, col - width + 2 * outer))
             for part in range(2):
-                window = dot(dot(pick_row, padded_ref[part]).astype(bf16), pick_col)
+                strips = [
+                    dot(pick_row, padded_ref[part, :, pl.ds(at, outer)]).astype(bf16)
+                    for at in (0, width - outer)
+                ]
+                window = dot(jnp.concatenate(strips, axis=1), pick_col)
                 out_ref[owner * slots + slot, part] = window.astype(bf16)
 
         @pl.when(owner != me)
@@ -301,8 +306,11 @@
     rs_ref[tile] = half_ref[share(tile, piece)]
     refs = (tile_ref, row_ref, col_ref)
 
+    def sender(step):
+        return lax.rem(me + 2 * owners - owners // 2 - step, owners)
+
     def build(index, carry):
-        _, col, _ = slot_place(refs, index // slots, index % slots, tile, per_dev)
+        _, col, _ = slot_place(refs, sender(index // slots), index % slots, tile, per_dev)
         where = pl.ds(pl.multiple_of(index * length, length), length)
         put_ref[where, :] = one_hot((length, width), 1, col + margin)
         return carry
@@ -319,27 +327,36 @@
     others(tile, n_tile, lambda other: gather_copy(other, tile).start())
 
     def place(step, carry):
-        owner = lax.rem(me + 2 * owners - owners // 2 - step, owners)
+        owner = sender(step)
 
         @pl.when(owner != me)
         def _():
             finish(window_copy)(owner)
 
         for slot in range(slots):
-            index = owner * slots + slot
             row, _, keep = slot_place(refs, owner, slot, tile, per_dev)
-            where = pl.ds(pl.multiple_of(index * length, length), length)
+            where = pl.ds(pl.multiple_of((step * slots + slot) * length, length), length)
             put_row = one_hot((rows, length), 0, row, keep)
             for part in range(2):
-                spread_ref[part, :, where] = dot(put_row, returned_ref[index, part]).astype(bf16)
+                spread_ref[part, :, where] = dot(put_row, returned_ref[owner * slots + slot, part]).astype(bf16)
         return carry
 
-    lax.fori_loop(0, owners, place, 0)
-
-    def fill(col, size):
-        where = pl.ds(col, size)
-        for part in range(2):
-            grid_ref[part, :, where] = dot(spread_ref[part], put_ref[:, where])
+    outer = 2 * length
+    grid_ref[:, :, pl.ds(outer, width - 2 * outer)] = jnp.zeros((2, rows, width - 2 * outer), f32)
+
+    def fill(first, last, add):
+        depth = pl.ds(first * slots * length, (last - first) * slots * length)
+        for col in (0, width - outer):
+            where = pl.ds(col, outer)
+            for part in range(2):
+                product = dot(spread_ref[part, :, depth], put_ref[depth, where])
+                grid_ref[part, :, where] = grid_ref[part, :, where] + product if add else product
+
+    early = 3 * owners // 4
+    lax.fori_loop(0, early, place, 0)
+    fill(0, early, False)
+    lax.fori_loop(early, owners, place, 0)
+    fill(early, owners, True)
 
     def region(ref, dt, ds):
         return margin_part(ref, dt, ds, tile_rows, tile_cols, margin, length)
@@ -360,10 +377,7 @@
                 there, copy = margin_copy(number, 1)
                 pl.when(there > 0)(copy.start)
 
-    fill(0, 2 * length)
-    fill(width - 2 * length, 2 * length)
     send_margins(True)
-    fill(2 * length, width - 4 * length)
     send_margins(False)
     others(tile, n_tile, finish(gather_copy))
     others(mode, n_mode, lambda other: join_copy(other, mode).start())
@@ -425,22 +439,42 @@
     return (sum(p[0] for p in pairs[1:]) + pairs[0][0], sum(p[1] for p in pairs[1:]) + pairs[0][1])
 
 
-def position_terms(front, rear, probes, observed, tables, prop):
-    length = observed.shape[0]
+def position_terms(fronts, rears, probes, observed, tables, prop):
+    length = observed[0].shape[0]
+    modes = len(probes)
     ahead, behind = tables
     forward = lambda f: transform(f, ahead, behind, length)
     inverse = lambda f: transform(f, behind, ahead, length)
-    spec = forward([mul(p, front) for p in probes])
+    each = range(len(fronts) * modes)
+    front = lambda i: fronts[i // modes]()
+    rear = lambda i: rears[i // modes]()
+    probe = lambda i: probes[i % modes]
+    spec = forward([mul(probe(i), front(i)) for i in each])
     inner = inverse([mul(s, prop) for s in spec])
-    far = forward([mul(s, rear) for s in inner])
-    intensity = sum(re * re + im * im for re, im in far[1:]) + far[0][0] ** 2 + far[0][1] ** 2
-    factor = 1.0 - jnp.sqrt(observed) / jnp.sqrt(intensity + 1.0)
-    back_b = inverse([(re * factor, im * factor) for re, im in far])
-    back_spec = forward([conj_mul(rear, b) for b in back_b])
+    far = forward([mul(inner[i], rear(i)) for i in each])
+    resid = []
+    for q, seen in enumerate(observed):
+        mine = far[q * modes : (q + 1) * modes]
+        intensity = sum(re * re + im * im for re, im in mine[1:]) + mine[0][0] ** 2 + mine[0][1] ** 2
+        factor = 1.0 - jnp.sqrt(seen) / jnp.sqrt(intensity + 1.0)
+        resid += [(re * factor, im * factor) for re, im in mine]
+    back_b = inverse(resid)
+    back_spec = forward([conj_mul(rear(i), back_b[i]) for i in each])
     back_a = inverse([conj_mul(prop, b) for b in back_spec])
-    grad_a = total([conj_mul(p, b) for p, b in zip(probes, back_a)])
-    grad_b = total([conj_mul(s, b) for s, b in zip(inner, back_b)])
-    return grad_a, grad_b, [conj_mul(front, b) for b in back_a]
+    grads = []
+    for q in range(len(fronts)):
+        mine = range(q * modes, (q + 1) * modes)
+        grads.append(
+            (
+                total([conj_mul(probe(i), back_a[i]) for i in mine]),
+                total([conj_mul(inner[i], back_b[i]) for i in mine]),
+            )
+        )
+    terms = [
+        total([conj_mul(fronts[q](), back_a[q * modes + m]) for q in range(len(fronts))])
+        for m in range(modes)
+    ]
+    return grads, terms
 
 
 def position_kernel(n_tile, n_mode, slots, tile_ref, arrived_ref, probe_ref, meas_ref, table_ref, prop_ref, back_ref, pgrad_ref):
@@ -448,24 +482,30 @@
     modes = probe_ref.shape[1]
     owner = lax.axis_index("tile") * n_mode + lax.axis_index("mode")
     tiles, order = ranks(tile_ref, owner * per_dev, per_dev)
-    tables = (table_ref[0], table_ref[1])
     back_ref[...] = jnp.zeros_like(back_ref)
+    place = [
+        [(tiles[q] * n_mode + k * n_mode // 2) * slots + order[q] for k in range(2)]
+        for q in range(per_dev)
+    ]
+
+    def window(q, k):
+        return lambda: tuple(arrived_ref[place[q][k], part].astype(f32) for part in range(2))
+
+    grads, terms = position_terms(
+        [window(q, 0) for q in range(per_dev)],
+        [window(q, 1) for q in range(per_dev)],
+        [(probe_ref[0, m], probe_ref[1, m]) for m in range(modes)],
+        [meas_ref[q] for q in range(per_dev)],
+        (table_ref[0], table_ref[1]),
+        (prop_ref[0], prop_ref[1]),
+    )
     for q in range(per_dev):
-        place = [(tiles[q] * n_mode + k * n_mode // 2) * slots + order[q] for k in range(2)]
-        pair = lambda k: (arrived_ref[place[k], 0].astype(f32), arrived_ref[place[k], 1].astype(f32))
-        probes = [(probe_ref[0, m], probe_ref[1, m]) for m in range(modes)]
-        grad_a, grad_b, terms = position_terms(
-            pair(0), pair(1), probes, meas_ref[q], tables, (prop_ref[0], prop_ref[1])
-        )
-        for k, grad in enumerate((grad_a, grad_b)):
+        for k in range(2):
             for part in range(2):
-                back_ref[place[k], part] = grad[part].astype(bf16)
-        for m, term in enumerate(terms):
-            for part in range(2):
-                if q == 0:
-                    pgrad_ref[part, m] = term[part]
-                else:
-                    pgrad_ref[part, m] += term[part]
+                back_ref[place[q][k], part] = grads[q][k][part].astype(bf16)
+    for m in range(modes):
+        for part in range(2):
+            pgrad_ref[part, m] = terms[m][part]
 
 
 smem = pl.BlockSpec(memory_space=pltpu.SMEM)

time: 90.8 us -> 85.2 us (0.938)
  Pallas kernels: 86.8 us -> 81.2 us
    pallas_call x1, Pallas kernels: 8.67 us -> 3.46 us  [on_device(): pl.pallas_call(lambda *refs: position_kernel(n_tile, n_mode, slots, *refs...]
where the time goes in v4:
time: 85.2 us; the launch traced here: 85 us
  Pallas kernels  81.2 us (95%)
  local copies, waits for them, and re-layouts  3.13 us (4%)
    pallas_call x1, Pallas kernels, on_device(): pl.pallas_call(lambda *refs: backward_kernel(*sizes, *refs), out_shape=(j...  41.6 us
    pallas_call x1, Pallas kernels, on_device(): pl.pallas_call(lambda *refs: forward_kernel(*sizes, *refs), out_shape=win...  36.1 us
    pallas_call x1, Pallas kernels, on_device(): pl.pallas_call(lambda *refs: position_kernel(n_tile, n_mode, slots, *refs...  3.46 us
    unnamed x18, local copies, waits for them, and re-layouts  3.13 us

profile of v4, /device:TPU:0, one launch (start us, length us, event | category | flops | bytes accessed | tf_op | source)
XLA Modules:
  0.0 85.0 jit_solution(17128513531771607238)
XLA Ops:
  0.6 0.0 copy-start.5
  0.6 0.0 copy-start.6
  0.7 0.0 copy-start.7
  0.7 0.6 copy-done.5
  1.3 0.0 copy-done.6
  1.3 0.0 copy-done.7
  1.3 0.0 copy-start.3
  1.3 0.9 %copy-done.3 = bf16[2,1,128,512]{3,2,1,0:T(8,128)(2,1)S(1)} copy-done((bf16[2,1,128,512]{3,2,1,0:T(8,128)(2,1)S(1)}, bf16[2,1,128,512]{3,2,1,0:T(8,128)(2,1)}, u32[]{:S(2)}) %copy-start.3) | copy-done | bytes 262168
  2.3 0.0 copy-start
  2.3 0.0 copy-start.1
  2.3 0.0 copy-start.2
  2.3 0.0 copy-start.4
  2.3 36.1 %forward.1.refs_1_ = bf16[16,2,128,128]{3,2,1,0:T(8,128)(2,1)S(1)} custom-call(s32[32]{0:T(128)S(1)} %bitcast.15, s32[32]{0:T(128)S(1)} %bitcast.18, s32[32]{0:T(128)S(1)} %bitcast.20, bf16[2,128,512]{2,1,0:T(8,128)(2,1)S(1)} %bitcast.13), custom_call_target="tpu_custom_call" | custom-call | tf_op jit(solution)/shard_map/forward/pallas_call | solution.py:540
  38.4 0.0 copy-done
  38.4 0.0 copy-done.1
  38.4 0.0 copy-done.2
  38.4 0.0 copy-done.4
  38.4 3.5 %positions.1 = (bf16[16,2,128,128]{3,2,1,0:T(8,128)(2,1)S(1)}, f32[2,2,128,128]{3,2,1,0:T(8,128)S(1)}) custom-call(s32[32]{0:T(128)S(1)} %bitcast.16, bf16[16,2,128,128]{3,2,1,0:T(8,128)(2,1)S(1)} %forward.1.refs_1_, f32[2,2,128,128]{3,2,1,0:T(8,128)S(1)} %copy-done, f32[4,128,128]{2,1,0:T(8,128)S(1)} %bitcast.11, bf16[2,256,256]{2,1,0:T(8,128)(2,1)S(1)} %copy-done.2, ...), custom_call_target="tpu_custom_call" | custom-call | tf_op jit(solution)/shard_map/positions/pallas_call | solution.py:554
  41.9 41.6 %backward.1 = (f32[2,128,512]{2,1,0:T(8,128)S(1)}, f32[512,128]{1,0:T(8,128)S(1)}) custom-call(s32[32]{0:T(128)S(1)} %bitcast.17, s32[32]{0:T(128)S(1)} %bitcast.19, s32[32]{0:T(128)S(1)} %bitcast.21, bf16[16,2,128,128]{3,2,1,0:T(8,128)(2,1)S(1)} %get-tuple-element.6.refs_3_, f32[512,128]{1,0:T(8,128)S(1)} %bitcast.14), custom_call_target="tpu_custom_call" | custom-call | tf_op jit(solution)/shard_map/backward/pallas_call | solution.py:564
  83.5 0.8 copy.13
  84.3 0.7 copy.14
Async XLA Ops:
  0.6 0.7 copy-start.5
  0.6 0.7 copy-start.6
  0.7 0.7 copy-start.7
  1.3 0.9 %copy-start.3 = (bf16[2,1,128,512]{3,2,1,0:T(8,128)(2,1)S(1)}, bf16[2,1,128,512]{3,2,1,0:T(8,128)(2,1)}, u32[]{:S(2)}) copy-start(bf16[2,1,128,512]{3,2,1,0:T(8,128)(2,1)} %param.8) | copy-start | bytes 786436
  2.3 36.1 %copy-start = (f32[2,2,128,128]{3,2,1,0:T(8,128)S(1)}, f32[2,2,128,128]{3,2,1,0:T(8,128)}, u32[]{:S(2)}) copy-start(f32[2,2,128,128]{3,2,1,0:T(8,128)} %refs_2_.1) | copy-start | bytes 786436
  2.3 36.1 %copy-start.1 = (f32[1,4,128,128]{3,2,1,0:T(8,128)S(1)}, f32[1,4,128,128]{3,2,1,0:T(8,128)}, u32[]{:S(2)}) copy-start(f32[1,4,128,128]{3,2,1,0:T(8,128)} %param.10) | copy-start | bytes 786436
  2.3 36.1 %copy-start.2 = (bf16[2,256,256]{2,1,0:T(8,128)(2,1)S(1)}, bf16[2,256,256]{2,1,0:T(8,128)(2,1)}, u32[]{:S(2)}) copy-start(bf16[2,256,256]{2,1,0:T(8,128)(2,1)} %constant.11.refs_4_) | copy-start | bytes 786436
  2.3 36.1 %copy-start.4 = (f32[2,128,128]{2,1,0:T(8,128)S(1)}, f32[2,128,128]{2,1,0:T(8,128)}, u32[]{:S(2)}) copy-start(f32[2,128,128]{2,1,0:T(8,128)} %constant.5.clone.refs_5_) | copy-start | bytes 393220

commit v5 on v4

--- a/solution.py
+++ b/solution.py
@@ -297,12 +297,26 @@
         return act
 
     others(mode, n_mode, lambda other: pair_copy(other, mode).start())
-    others(me, owners, lambda other: window_copy(other, me).start())
+
+    def send_windows(first, last):
+        def body(step, carry):
+            other = lax.rem(me + owners // 2 + step, owners)
+
+            @pl.when(other != me)
+            def _():
+                window_copy(other, me).start()
+
+            return carry
+
+        lax.fori_loop(first, last, body, 0)
+
+    send_windows(0, 1)
     pair_ref[mode] = part_ref[share(mode, half)]
     returned_ref[span(me)] = back_ref[span(me)]
     others(mode, n_mode, finish(pair_copy))
     half_ref[...] = lax.fori_loop(1, n_mode, lambda i, acc: acc + pair_ref[i], pair_ref[0])
     others(tile, n_tile, lambda other: reduce_copy(other, tile).start())
+    send_windows(1, owners // 2)
     rs_ref[tile] = half_ref[share(tile, piece)]
     refs = (tile_ref, row_ref, col_ref)
 
@@ -325,6 +339,7 @@
         1, n_strip, lambda i, acc: acc + strip_ref[i], strip_ref[0]
     )
     others(tile, n_tile, lambda other: gather_copy(other, tile).start())
+    send_windows(owners // 2, owners)
 
     def place(step, carry):
         owner = sender(step)

time: 85.2 us -> 86 us (level)
  no operation moved by 1% of the time
where the time goes in v5:
time: 86 us; the launch traced here: 85.8 us
  Pallas kernels  81.9 us (95%)
  local copies, waits for them, and re-layouts  3.13 us (4%)
    pallas_call x1, Pallas kernels, on_device(): pl.pallas_call(lambda *refs: backward_kernel(*sizes, *refs), out_shape=(j...  42.4 us
    pallas_call x1, Pallas kernels, on_device(): pl.pallas_call(lambda *refs: forward_kernel(*sizes, *refs), out_shape=win...  36.1 us
    pallas_call x1, Pallas kernels, on_device(): pl.pallas_call(lambda *refs: position_kernel(n_tile, n_mode, slots, *refs...  3.46 us
    unnamed x18, local copies, waits for them, and re-layouts  3.13 us

profile of v5, /device:TPU:0, one launch (start us, length us, event | category | flops | bytes accessed | tf_op | source)
XLA Modules:
  0.0 85.8 jit_solution(737481265238719402)
XLA Ops:
  0.6 0.0 copy-start.5
  0.6 0.0 copy-start.6
  0.7 0.0 copy-start.7
  0.7 0.6 copy-done.5
  1.3 0.0 copy-done.6
  1.3 0.0 copy-done.7
  1.3 0.0 copy-start.3
  1.3 0.9 %copy-done.3 = bf16[2,1,128,512]{3,2,1,0:T(8,128)(2,1)S(1)} copy-done((bf16[2,1,128,512]{3,2,1,0:T(8,128)(2,1)S(1)}, bf16[2,1,128,512]{3,2,1,0:T(8,128)(2,1)}, u32[]{:S(2)}) %copy-start.3) | copy-done | bytes 262168
  2.3 0.0 copy-start
  2.3 0.0 copy-start.1
  2.3 0.0 copy-start.2
  2.3 0.0 copy-start.4
  2.3 36.1 %forward.1.refs_1_ = bf16[16,2,128,128]{3,2,1,0:T(8,128)(2,1)S(1)} custom-call(s32[32]{0:T(128)S(1)} %bitcast.15, s32[32]{0:T(128)S(1)} %bitcast.18, s32[32]{0:T(128)S(1)} %bitcast.20, bf16[2,128,512]{2,1,0:T(8,128)(2,1)S(1)} %bitcast.13), custom_call_target="tpu_custom_call" | custom-call | tf_op jit(solution)/shard_map/forward/pallas_call | solution.py:555
  38.4 0.0 copy-done
  38.4 0.0 copy-done.1
  38.4 0.0 copy-done.2
  38.4 0.0 copy-done.4
  38.4 3.5 %positions.1 = (bf16[16,2,128,128]{3,2,1,0:T(8,128)(2,1)S(1)}, f32[2,2,128,128]{3,2,1,0:T(8,128)S(1)}) custom-call(s32[32]{0:T(128)S(1)} %bitcast.16, bf16[16,2,128,128]{3,2,1,0:T(8,128)(2,1)S(1)} %forward.1.refs_1_, f32[2,2,128,128]{3,2,1,0:T(8,128)S(1)} %copy-done, f32[4,128,128]{2,1,0:T(8,128)S(1)} %bitcast.11, bf16[2,256,256]{2,1,0:T(8,128)(2,1)S(1)} %copy-done.2, ...), custom_call_target="tpu_custom_call" | custom-call | tf_op jit(solution)/shard_map/positions/pallas_call | solution.py:569
  41.9 42.4 %backward.1 = (f32[2,128,512]{2,1,0:T(8,128)S(1)}, f32[512,128]{1,0:T(8,128)S(1)}) custom-call(s32[32]{0:T(128)S(1)} %bitcast.17, s32[32]{0:T(128)S(1)} %bitcast.19, s32[32]{0:T(128)S(1)} %bitcast.21, bf16[16,2,128,128]{3,2,1,0:T(8,128)(2,1)S(1)} %get-tuple-element.6.refs_3_, f32[512,128]{1,0:T(8,128)S(1)} %bitcast.14), custom_call_target="tpu_custom_call" | custom-call | tf_op jit(solution)/shard_map/backward/pallas_call | solution.py:579
  84.3 0.8 copy.13
  85.1 0.7 copy.14
Async XLA Ops:
  0.6 0.7 copy-start.5
  0.6 0.7 copy-start.6
  0.7 0.7 copy-start.7
  1.3 0.9 %copy-start.3 = (bf16[2,1,128,512]{3,2,1,0:T(8,128)(2,1)S(1)}, bf16[2,1,128,512]{3,2,1,0:T(8,128)(2,1)}, u32[]{:S(2)}) copy-start(bf16[2,1,128,512]{3,2,1,0:T(8,128)(2,1)} %param.8) | copy-start | bytes 786436
  2.3 36.1 %copy-start = (f32[2,2,128,128]{3,2,1,0:T(8,128)S(1)}, f32[2,2,128,128]{3,2,1,0:T(8,128)}, u32[]{:S(2)}) copy-start(f32[2,2,128,128]{3,2,1,0:T(8,128)} %refs_2_.1) | copy-start | bytes 786436
  2.3 36.1 %copy-start.1 = (f32[1,4,128,128]{3,2,1,0:T(8,128)S(1)}, f32[1,4,128,128]{3,2,1,0:T(8,128)}, u32[]{:S(2)}) copy-start(f32[1,4,128,128]{3,2,1,0:T(8,128)} %param.10) | copy-start | bytes 786436
  2.3 36.1 %copy-start.2 = (bf16[2,256,256]{2,1,0:T(8,128)(2,1)S(1)}, bf16[2,256,256]{2,1,0:T(8,128)(2,1)}, u32[]{:S(2)}) copy-start(bf16[2,256,256]{2,1,0:T(8,128)(2,1)} %constant.11.refs_4_) | copy-start | bytes 786436
  2.3 36.1 %copy-start.4 = (f32[2,128,128]{2,1,0:T(8,128)S(1)}, f32[2,128,128]{2,1,0:T(8,128)}, u32[]{:S(2)}) copy-start(f32[2,128,128]{2,1,0:T(8,128)} %constant.5.clone.refs_5_) | copy-start | bytes 393220
